TPU v7x, 512 devices: a whole 4x8x8 slice. The times are simulated.
512 devices in a mesh: row: 32 (over z, x_lo, core), rep: 16 (over x_hi, y).
Axes of the slice: x: 4 (x_hi: 2, x_lo: 2; x = x_hi * 2 + x_lo), y: 8, z: 8, core: 2. Of those that a mesh axis runs over, the one named last changes fastest.
Arguments:
- feats: bfloat16 [32768, 256], P('row'), may hold values from -6 to 6
- weight: bfloat16 [256, 256], replicated, may hold values from -0.375 to 0.375
- weight_mask: int32 [256, 256], replicated, may hold values 0 or 1
- tile_vals: bfloat16 [6144, 128, 128], P(('row', 'rep')), may hold values from -0.109375 to 0.109375
- edge_mask: float32 [6144, 128, 128], P(('row', 'rep')), may hold values from 0.25 to 2
- tile_pos: int32 [6144], P(('row', 'rep')), may hold values from -1 to 127, as said below
- grad_out: bfloat16 [32768, 256], P('row'), may hold values from -6 to 6
Outputs:
- out_feats: bfloat16 [32768, 256], P('row')
- feature_gradient: bfloat16 [32768, 256], P('row')
- weight_gradient: float32 [256, 256], replicated
- grad_edge: float32 [6144, 128, 128], P(('row', 'rep'))
Inputs may be any that keep to these rules, and one draw needn't show every extreme that they name: `tile_pos`: entries of one device (d * 12 onward) hold distinct tile positions below 128 first and -1 after them; at least one entry of every device is live, and some device has all 12 live.
All inputs are finite; a program needn't handle non-finite values.
Results may differ from a plain program's by a relative error of at most 0.0058.
Values may be sent and summed in bfloat16 or wider, within the bound.
A program may use at most 64 MiB of HBM per device.

v0:
```python
import jax
import jax.numpy as jnp
from jax import lax
from jax.sharding import PartitionSpec as P


def spread(block, axis, holder):
    block = jnp.where(lax.axis_index(axis) == holder, block, jnp.zeros_like(block))
    return lax.psum(block, axis)


def on_device(feats, weight, weight_mask, tile_vals, edge_mask, tile_pos, grad_out):
    rep_count = lax.axis_size("rep")
    row_count = lax.axis_size("row")
    rep_index = lax.axis_index("rep")
    row_index = lax.axis_index("row")
    block, width = feats.shape
    side = tile_vals.shape[1]
    per_side = block // side
    sections = row_count // rep_count
    w_eff = jnp.where(weight_mask != 0, weight, jnp.zeros_like(weight))
    proj = jnp.dot(feats, w_eff, preferred_element_type=jnp.float32).astype(jnp.bfloat16)
    received = []
    for section in range(sections):
        received.append(spread(proj, "row", section * rep_count + rep_index))
    col_blocks = jnp.stack(received).reshape(sections * per_side, side, width)
    live = tile_pos >= 0
    slot = jnp.maximum(tile_pos, 0)
    col_pick = slot // (per_side * per_side) * per_side + slot % per_side
    row_pick = slot // per_side % per_side
    col_tiles = col_blocks[col_pick]
    masked = (tile_vals.astype(jnp.float32) * edge_mask).astype(jnp.bfloat16)
    contrib = jnp.einsum("tab,tbf->taf", masked, col_tiles, preferred_element_type=jnp.float32)
    row_onehot = ((row_pick[None, :] == jnp.arange(per_side)[:, None]) & live[None, :]).astype(
        jnp.float32
    )
    partial_out = jnp.einsum(
        "rt,taf->raf", row_onehot, contrib, precision=lax.Precision.HIGHEST
    ).reshape(block, width)
    out_feats = lax.psum(partial_out, "rep").astype(jnp.bfloat16)
    tile_gradients = grad_out.reshape(per_side, side, width)
    row_tiles = tile_gradients[row_pick]
    scores = jnp.einsum("taf,tbf->tab", row_tiles, col_tiles, preferred_element_type=jnp.float32)
    grad_edge = jnp.where(live[:, None, None], tile_vals.astype(jnp.float32) * scores, 0.0)
    backward_result = jnp.einsum(
        "tab,taf->tbf", masked, row_tiles, preferred_element_type=jnp.float32
    )
    column_indicator = (
        (col_pick[None, :] == jnp.arange(sections * per_side)[:, None]) & live[None, :]
    ).astype(jnp.float32)
    col_terms = jnp.einsum(
        "qa,amp->qmp", column_indicator, backward_result, precision=lax.Precision.HIGHEST
    ).reshape(sections, block, width)
    owned = jnp.zeros((block, width), jnp.bfloat16)
    for section in range(sections):
        summed = lax.psum(col_terms[section], "row").astype(jnp.bfloat16)
        is_owner = row_index == section * rep_count + rep_index
        owned = jnp.where(is_owner, summed, owned)
    grad_cols = spread(owned, "rep", row_index % rep_count)
    feature_gradient = lax.dot_general(
        grad_cols, w_eff, (((1,), (1,)), ((), ())), preferred_element_type=jnp.float32
    ).astype(jnp.bfloat16)
    partial_weight = lax.dot_general(
        feats, grad_cols, (((0,), (0,)), ((), ())), preferred_element_type=jnp.float32
    )
    total_weight = lax.psum(partial_weight, "row")
    weight_gradient = jnp.where(weight_mask != 0, total_weight, jnp.zeros_like(total_weight))
    return (out_feats, feature_gradient, weight_gradient, grad_edge)


def solution(mesh):
    placed = (
        P("row", None),
        P(),
        P(),
        P(("row", "rep"), None, None),
        P(("row", "rep"), None, None),
        P(("row", "rep")),
        P("row", None),
    )
    return jax.shard_map(
        on_device,
        mesh=mesh,
        in_specs=placed,
        out_specs=(P("row", None), P("row", None), P(), P(("row", "rep"), None, None)),
        check_vma=False,
    )
```

profile of v0, /device:TPU:1, one launch (start us, length us, event | category | flops | bytes accessed | tf_op | source)
XLA Modules:
  0.0 867.6 jit_solution(9729874776296867352)
XLA Ops:
  7.3 0.8 compare_select_fusion.1
  8.0 0.7 broadcast_compare_fusion.1
  8.7 0.6 gather_fusion.1
  9.4 0.4 fusion.24
  9.8 2.0 fusion
  11.9 0.3 copy.18
  12.3 0.3 copy.19
  12.6 133.9 %all-reduce.13 = (bf16[1024,256]{1,0:T(8,128)(2,1)}, bf16[1024,256]{1,0:T(8,128)(2,1)}) all-reduce(f32[1024,256]{1,0:T(8,128)S(1)} %bitcast.31, f32[1024,256]{1,0:T(8,128)S(1)} %bitcast.30), channel_id=1, replica_groups=mesh['row'=32,'rep'=16] {'row'}, use_global_device_ids=true, to_apply=%region_4.5 | all-reduce | flops 524288 | bytes 3145728 | tf_op jit(solution)/shard_map/psum | solution.py:56
  146.6 0.9 select_select_fusion
  147.5 151.8 %all-reduce.8.cloned.1.call-done = bf16[1024,256]{1,0:T(8,128)(2,1)} async-done(((bf16[1024,256]{1,0:T(8,128)(2,1)}), bf16[1024,256]{1,0:T(8,128)(2,1)}) %all-reduce.8.cloned.1.call-update) | async-done | bytes 524304 | tf_op jit(solution)/shard_map/psum | solution.py:9
  299.3 2.1 convolution_bitcast_fusion
  301.7 237.5 %all-reduce.10.cloned.1.call-done = f32[256,256]{0,1:T(8,128)} async-done(((f32[256,256]{0,1:T(8,128)}), f32[256,256]{0,1:T(8,128)}) %all-reduce.10.cloned.1.call-update) | async-done | bytes 262160 | tf_op jit(solution)/shard_map/psum | solution.py:66
  539.2 1.0 broadcast_select_fusion
  540.2 1.3 select_bitcast_fusion.1
  541.5 0.8 copy.20
  542.4 1.1 convolution_convert_fusion
  543.4 232.4 %all-reduce.12.cloned.1.call-done = (bf16[1,1024,256]{1,2,0:T(8,128)(2,1)}, bf16[1,1024,256]{1,2,0:T(8,128)(2,1)}) async-done(((bf16[1,1024,256]{1,2,0:T(8,128)(2,1)}, bf16[1,1024,256]{1,2,0:T(8,128)(2,1)}), (bf16[1,1024,256]{1,2,0:T(8,128)(2,1)}, bf16[1,1024,256]{1,2,0:T(8,128)(2,1)})) %all-reduce.12.cloned.1.call-update) | async-done | bytes 1048592 | tf_op jit(solution)/shard_map/psum | solution.py:9
  775.9 1.3 pad_maximum_fusion
  777.2 1.3 copy.16
  778.5 1.8 gather_fusion
  780.3 0.4 fusion.26
  780.7 1.3 fusion.4
  781.9 1.7 fusion.2
  784.0 77.1 %all-reduce.14 = bf16[1024,256]{1,0:T(8,128)(2,1)} all-reduce(f32[1024,256]{1,0:T(8,128)S(1)} %bitcast.32), channel_id=1, replica_groups=mesh['row'=32,'rep'=16] {'rep'}, use_global_device_ids=true, to_apply=%region_2.3 | all-reduce | flops 262144 | bytes 1572864 | tf_op jit(solution)/shard_map/psum | solution.py:40
  (29 shorter events, 1.0 us)
Async XLA Ops:
  7.2 1.6 copy-start
  7.2 2.2 copy-start.1
  7.2 2.2 copy-start.3
  7.2 292.1 %all-reduce.8.cloned.1.call-start = ((), (), s32[]{:S(2)}) async-start(), calls=%async_computation | async-start | bytes 1048576 | tf_op jit(solution)/shard_map/psum | solution.py:9
  146.6 152.7 %copy-start.5 = (bf16[1024,256]{1,0:T(8,128)(2,1)S(1)}, bf16[1024,256]{1,0:T(8,128)(2,1)}, u32[]{:S(2)}) copy-start(bf16[1024,256]{1,0:T(8,128)(2,1)} %param.7) | copy-start | bytes 1572868
  146.6 154.9 %copy-start.7 = (s32[256,256]{1,0:T(8,128)S(1)}, s32[256,256]{1,0:T(8,128)}, u32[]{:S(2)}) copy-start(s32[256,256]{1,0:T(8,128)} %param.9) | copy-start | bytes 786436
  147.4 154.2 %copy-start.8 = (bf16[256,256]{1,0:T(8,128)(2,1)S(1)}, bf16[256,256]{1,0:T(8,128)(2,1)}, u32[]{:S(2)}) copy-start(bf16[256,256]{1,0:T(8,128)(2,1)} %param.8) | copy-start | bytes 393220
  147.4 391.7 %all-reduce.10.cloned.1.call-start = ((), (), s32[]{:S(2)}) async-start(), calls=%async_computation.1 | async-start | bytes 524288 | tf_op jit(solution)/shard_map/psum | solution.py:66
  301.4 474.5 %all-reduce.12.cloned.1.call-start = ((), (), s32[]{:S(2)}) async-start(), calls=%async_computation.2 | async-start | bytes 2097152 | tf_op jit(solution)/shard_map/psum | solution.py:9
  540.2 2.2 copy-start.6
  777.2 3.2 copy-start.2
  777.2 3.1 copy-start.4
Sparse Core Ops, SparseCore 0:
  147.6 151.6 all-reduce.7
  303.0 236.1 all-reduce.9
  542.7 233.1 all-reduce.11
where the time goes:
time: 877 us; the launch traced here: 868 us
  waiting for transfers between devices  622 us (71%)
  blocking collectives  211 us (24%)
  between operations  14 us (2%)
  matrix products  10.1 us (1%)
    psum x2, waiting for transfers between devices, spread(): return lax.psum(block, axis)  384 us
    psum x1, waiting for transfers between devices, on_device(): total_weight = lax.psum(partial_weight, 'row')  237 us
    psum x1, blocking collectives, on_device(): summed = lax.psum(col_terms[section], 'row').astype(jnp.bfloat16)  134 us
    psum x1, blocking collectives, on_device(): out_feats = lax.psum(partial_out, 'rep').astype(jnp.bfloat16)  77.1 us
  transfers between devices with their start and end apart: 3, of which 3 were waited for; matrix products, arithmetic and copies ran while one was open for 0% of the time, Pallas kernels for 0%

commit v1 on v0

v1 whole, which is shorter than its diff:
```python
import functools

import jax
import jax.numpy as jnp
from jax import lax
from jax.experimental import pallas as pl
from jax.experimental.pallas import tpu as pltpu
from jax.sharding import PartitionSpec as P

BF = jnp.bfloat16
F32 = jnp.float32


def semaphore_places(n):
    counts = dict(
        a1=2, a2=n, a3=n, a4=2 * n,
        d1=2 * n, d2=n, d3=n, d4=2, d5=n, d6=n,
        c1=n, c2=n, c3=n, c4=n,
        wz=n, wc=4, wy=n, wx=n,
    )
    places, total = {}, 0
    for name, count in counts.items():
        places[name] = total
        total += count
    return places, total


def loop(low, high, step):
    def run(i, carry):
        step(i)
        return carry

    lax.fori_loop(low, high, run, 0)


def kernel(
    n, places,
    pos_ref, feats_h, gout_h, w_h, wm_h, tv_h, em_h,
    out_h, fg_h, wg_h, ge_h,
    feats, gout, w, wm, tv, em,
    weff, a1s, pj, mk, mkt, gs, rs, lhs, pb,
    d1r, d2s, d2r, d3s, d3r, d3o, d4s, gc,
    yb, c1r, c2s, c2r, c2o, oc,
    ft, wp, wz, wc, wa, wgo, ge, fg,
    send, recv, local,
):
    row, rep = lax.axis_index("row"), lax.axis_index("rep")
    z, xl, c = row // 4, row // 2 % 2, row % 2
    xh, y = rep // n, rep % n
    reps = 2 * n
    tiles, side, _ = tv.shape
    width = w.shape[0]
    piece_rows = pj.shape[2]
    per_side = gout.shape[0]
    ppt = side // piece_rows
    block = per_side * side

    def row_of(zz, xx, cc):
        return zz * 4 + xx * 2 + cc

    core_row, lo_row, both_row = row_of(z, xl, 1 - c), row_of(z, 1 - xl, c), row_of(z, 1 - xl, 1 - c)
    hi_rep = (1 - xh) * n + y
    mine = (c * 2 + xl) * n + z

    def around(at, o):
        return lax.rem(at + o, n)

    def copy(name, i, j, src, dst, to_row, to_rep):
        return pltpu.make_async_remote_copy(
            src_ref=src,
            dst_ref=dst,
            send_sem=send.at[places[name] + i],
            recv_sem=recv.at[places[name] + j],
            device_id=(to_row, to_rep),
            device_id_type=pl.DeviceIdType.MESH,
        )

    def arrived(name, j, ref):
        copy(name, 0, j, ref, ref, core_row, rep).wait_recv()

    def left(name, i, ref):
        copy(name, i, 0, ref, ref, core_row, rep).wait_send()

    owner_rows, owner_rep = [k * reps + rep for k in range(2)], mine // 2
    own_half = lax.rem(mine, 2)
    section, group = row // reps, lax.rem(row, reps)
    part_rows, parts = [], []
    for e in range(2):
        p = 2 * rep + e
        parts.append(p)
        part_rows.append(row_of(lax.rem(p, n), lax.rem(p // n, 2), p // (2 * n)))

    def is_me(r, q):
        return jnp.logical_and(r == row, q == rep)

    ins = []
    for i, (src, dst) in enumerate(
        ((w_h, w), (wm_h, wm), (feats_h, feats), (tv_h, tv), (em_h, em), (gout_h, gout))
    ):
        ins.append(pltpu.make_async_copy(src, dst, local.at[i]))
        ins[-1].start()

    barrier = pltpu.get_barrier_semaphore()

    def greet(r, q):
        pl.semaphore_signal(barrier, inc=1, device_id=(r, q), device_id_type=pl.DeviceIdType.MESH)

    greet(core_row, rep)
    greet(lo_row, rep)
    greet(both_row, rep)
    greet(row, hi_rep)
    loop(1, n, lambda o: greet(row_of(around(z, o), xl, c), rep))
    loop(1, n, lambda o: greet(row, xh * n + around(y, o)))
    expected = 4 + 2 * (n - 1)
    for k in range(2):
        for r, q in ((owner_rows[k], owner_rep), (part_rows[k], group)):
            other = jnp.logical_not(is_me(r, q))
            pl.when(other)(functools.partial(greet, r, q))
            expected = expected + other.astype(jnp.int32)

    ins[0].wait()
    ins[1].wait()
    weff[...] = jnp.where(wm[...] != 0, w[...].astype(F32), 0.0).astype(BF)
    ins[2].wait()
    piece = jnp.dot(feats[rep], weff[...], preferred_element_type=F32).astype(BF)
    a1s[...] = piece.reshape(a1s.shape)

    pl.semaphore_wait(barrier, expected)

    def scatter_piece(e):
        src, dst = a1s.at[e], pj.at[parts[e], section]
        same = is_me(part_rows[e], group)

        @pl.when(jnp.logical_not(same))
        def _():
            copy("a1", e, section, src, dst, part_rows[e], group).start()

        @pl.when(same)
        def _():
            pltpu.make_async_copy(src, dst, recv.at[places["a1"] + section]).start()

    scatter_piece(0)
    scatter_piece(1)

    picks = []
    for t in range(tiles):
        pos = pos_ref[t]
        slot = jnp.maximum(pos, 0)
        picks.append(
            (
                pos >= 0,
                lax.rem(slot // per_side, per_side),
                slot // (per_side * per_side),
                lax.rem(slot, per_side),
            )
        )

    ins[3].wait()
    ins[4].wait()
    ins[5].wait()
    for t in range(tiles):
        product = tv[t].astype(F32) * em[t]
        mk[t] = product.astype(BF)
        mkt[t] = product.T.astype(BF)
        gs[t] = gout[picks[t][1]]

    def chosen(cond, tile):
        return lax.select_n(cond, jnp.zeros_like(tile), tile)

    def backward_tile(jj):
        for k in range(2):
            for t in range(tiles):
                live, _, kt, jt = picks[t]
                cond = jnp.logical_and(live, jnp.logical_and(kt == k, jt == jj))
                lhs[k * side:(k + 1) * side, t * side:(t + 1) * side] = chosen(cond, mkt[t])
        total = jnp.dot(lhs[...], gs[...].reshape(tiles * side, width), preferred_element_type=F32)
        total = total.astype(BF)
        for k in range(2):
            pb[pl.ds(jj * ppt, ppt), k] = total[k * side:(k + 1) * side].reshape(ppt, piece_rows, width)

    quarter_tiles = n // ppt

    def send_quarter(x):
        def one(i):
            m = x * n + i
            copy("d1", m, m, pb.at[(1 - c) * 2 * n + m], d1r.at[m], core_row, rep).start()

        first = ((1 - c) * 2 + x) * quarter_tiles
        loop(0, quarter_tiles, lambda i: backward_tile(first + i))
        loop(0, n, one)

    send_quarter(1 - xl)
    send_quarter(xl)

    arrived("a1", 0, a1s.at[0])
    arrived("a1", 1, a1s.at[0])

    def pass_lo(zz):
        p = (c * 2 + xl) * n + zz
        copy("a3", zz, zz, pj.at[p], pj.at[p], lo_row, rep).start()

    def pass_core(m):
        p = c * 2 * n + m
        copy("a4", m, m, pj.at[p], pj.at[p], core_row, rep).start()

    def pass_z(o):
        zz = around(z, o)
        copy("a2", zz, z, pj.at[mine], pj.at[mine], row_of(zz, xl, c), rep).start()

    pass_lo(z)
    loop(1, n, pass_z)
    pass_core(xl * n + z)

    loop(0, 2 * quarter_tiles, lambda i: backward_tile(c * 2 * quarter_tiles + i))

    def d2_step(o):
        zz = around(z, o)
        m = (1 - xl) * n + zz
        arrived("d1", m, d1r.at[m])
        d2s[zz] = (pb[c * 2 * n + m].astype(F32) + d1r[m].astype(F32)).astype(BF)
        copy("d2", zz, zz, d2s.at[zz], d2r.at[zz], lo_row, rep).start()

    loop(1, n + 1, d2_step)

    def a2_step(o):
        zz = around(z, o)
        arrived("a2", zz, a2_like)
        pass_lo(zz)
        pass_core(xl * n + zz)

    a2_like = pj.at[mine]
    loop(1, n, a2_step)

    def d3_sum(zz):
        m = xl * n + zz
        arrived("d1", m, d1r.at[m])
        arrived("d2", zz, d2r.at[zz])
        return pb[c * 2 * n + m].astype(F32) + d1r[m].astype(F32) + d2r[zz].astype(F32)

    def d3_step(o):
        zz = around(z, o)
        d3s[zz] = d3_sum(zz).astype(BF)
        copy("d3", zz, z, d3s.at[zz], d3r.at[z], row_of(zz, xl, c), rep).start()

    loop(1, n, d3_step)
    d3o[...] = d3_sum(z)

    def a3_step(o):
        zz = around(z, o)
        arrived("a3", zz, a2_like)
        pass_core((1 - xl) * n + zz)

    loop(0, n, a3_step)

    def d3_add(o):
        zz = around(z, o)
        arrived("d3", zz, d3r.at[zz])
        d3o[...] += d3r[zz].astype(F32)

    loop(1, n, d3_add)
    d4s[...] = d3o[...].astype(BF)
    for k in range(2):
        same = is_me(owner_rows[k], owner_rep)
        src, dst = d4s.at[k], gc.at[owner_rep, own_half]

        @pl.when(jnp.logical_not(same))
        def _(src=src, dst=dst, k=k):
            copy("d4", k, own_half, src, dst, owner_rows[k], owner_rep).start()

        @pl.when(same)
        def _(src=src, dst=dst):
            pltpu.make_async_copy(src, dst, recv.at[places["d4"] + own_half]).start()

    loop(0, 2 * n, lambda m: arrived("a4", m, a2_like))

    for t in range(tiles):
        _, _, kt, jt = picks[t]
        rs[t] = pj[pl.ds(jt * ppt, ppt), kt].reshape(side, width)

    chunks_pair = 2 * side // (2 * piece_rows)
    pairs_half = block // 2 // (2 * side)

    def forward_pair(u):
        for h in range(2):
            for t in range(tiles):
                live, it, _, _ = picks[t]
                cond = jnp.logical_and(live, it == 2 * u + h)
                lhs[h * side:(h + 1) * side, t * side:(t + 1) * side] = chosen(cond, mk[t])
        total = jnp.dot(lhs[...], rs[...].reshape(tiles * side, width), preferred_element_type=F32)
        yb[pl.ds(u * chunks_pair, chunks_pair)] = total.astype(BF).reshape(
            chunks_pair, 2 * piece_rows, width
        )

    loop(0, pairs_half, lambda i: forward_pair((1 - xh) * pairs_half + i))

    def c1_step(o):
        yy = around(y, o)
        copy("c1", yy, yy, yb.at[(1 - xh) * n + yy], c1r.at[yy], row, hi_rep).start()

    loop(1, n + 1, c1_step)
    loop(0, pairs_half, lambda i: forward_pair(xh * pairs_half + i))

    def pass_hi(name, ref, yy):
        at = xh * n + yy
        copy(name, yy, yy, ref.at[at], ref.at[at], row, hi_rep).start()

    def pass_y(name, ref, o):
        yy = around(y, o)
        copy(name, yy, y, ref.at[rep], ref.at[rep], row, xh * n + yy).start()

    arrived("d4", 0, d4s.at[0])
    arrived("d4", 1, d4s.at[0])
    pass_hi("d6", gc, y)
    loop(1, n, lambda o: pass_y("d5", gc, o))

    def c2_sum(yy):
        arrived("c1", yy, c1r.at[yy])
        return yb[xh * n + yy].astype(F32) + c1r[yy].astype(F32)

    def c2_step(o):
        yy = around(y, o)
        c2s[yy] = c2_sum(yy).astype(BF)
        copy("c2", yy, y, c2s.at[yy], c2r.at[y], row, xh * n + yy).start()

    loop(1, n, c2_step)
    c2o[...] = c2_sum(y)

    def relay(got, gone, ref, o):
        yy = around(y, o)
        arrived(got, yy, ref.at[rep])
        pass_hi(gone, ref, yy)

    loop(1, n, lambda o: relay("d5", "d6", gc, o))

    def c2_add(o):
        yy = around(y, o)
        arrived("c2", yy, c2r.at[yy])
        c2o[...] += c2r[yy].astype(F32)

    loop(1, n, c2_add)
    oc[rep] = c2o[...].astype(BF)
    pass_hi("c4", oc, y)
    loop(1, n, lambda o: pass_y("c3", oc, o))

    for t in range(tiles):
        live = picks[t][0]
        scores = lax.dot_general(gs[t], rs[t], (((1,), (1,)), ((), ())), preferred_element_type=F32)
        ge[t] = chosen(live, tv[t].astype(F32) * scores)
    outs = [pltpu.make_async_copy(ge, ge_h, local.at[0])]
    outs[-1].start()
    cpt = side // (2 * piece_rows)
    for i in range(per_side):
        rows = feats[i * cpt:(i + 1) * cpt].reshape(side, width)
        ft[:, i * side:(i + 1) * side] = rows.astype(F32).T.astype(BF)

    loop(0, n, lambda yy: arrived("d6", yy, gc.at[rep]))
    grad_cols = gc[...].reshape(block, width)
    wp[...] = jnp.dot(ft[...], grad_cols, preferred_element_type=F32).reshape(wp.shape)
    wz[z] = wp[rep]

    def wz_step(o):
        zz = around(z, o)
        copy("wz", zz, z, wz.at[z], wz.at[z], row_of(zz, xl, c), rep).start()

    loop(1, n, wz_step)
    loop(1, n, lambda o: relay("c3", "c4", oc, o))

    fg[...] = lax.dot_general(
        gc[...].reshape(block, width), weff[...], (((1,), (1,)), ((), ())), preferred_element_type=F32
    ).astype(BF)
    outs.append(pltpu.make_async_copy(fg, fg_h, local.at[1]))
    outs[-1].start()

    loop(1, n, lambda o: arrived("wz", around(z, o), wz.at[z]))
    spot = xl * 2 + c
    wc[spot] = functools.reduce(jnp.add, [wz[i] for i in range(n)])
    for i, (r, s) in enumerate(
        ((core_row, xl * 2 + 1 - c), (lo_row, (1 - xl) * 2 + c), (both_row, (1 - xl) * 2 + 1 - c))
    ):
        copy("wc", s, spot, wc.at[spot], wc.at[spot], r, rep).start()

    loop(0, n, lambda yy: arrived("c4", yy, oc.at[rep]))
    outs.append(pltpu.make_async_copy(oc, out_h, local.at[2]))
    outs[-1].start()

    for i in range(1, 4):
        arrived("wc", lax.rem(spot + i, 4), wc.at[spot])
    wa[rep] = (wc[0] + wc[1]) + (wc[2] + wc[3])
    pass_hi("wx", wa, y)
    loop(1, n, lambda o: pass_y("wy", wa, o))
    loop(1, n, lambda o: relay("wy", "wx", wa, o))
    loop(0, n, lambda yy: arrived("wx", yy, wa.at[rep]))
    wgo[...] = jnp.where(wm[...] != 0, wa[...].reshape(width, width), 0.0)
    outs.append(pltpu.make_async_copy(wgo, wg_h, local.at[3]))
    outs[-1].start()

    for k in range(2):
        pl.when(jnp.logical_not(is_me(part_rows[k], group)))(functools.partial(left, "a1", k, a1s.at[0]))
        pl.when(jnp.logical_not(is_me(owner_rows[k], owner_rep)))(
            functools.partial(left, "d4", k, d4s.at[0])
        )

    def along_z(o):
        zz = around(z, o)
        left("a2", zz, a2_like)
        left("d3", zz, a2_like)
        left("wz", zz, wz.at[z])

    def along_y(o):
        yy = around(y, o)
        left("d5", yy, gc.at[rep])
        left("c2", yy, oc.at[rep])
        left("c3", yy, oc.at[rep])
        left("wy", yy, wa.at[rep])

    def across(i):
        left("a3", i, a2_like)
        left("d2", i, a2_like)
        left("d6", i, gc.at[rep])
        left("c1", i, oc.at[rep])
        left("c4", i, oc.at[rep])
        left("wx", i, wa.at[rep])

    def cores(m):
        left("a4", m, a2_like)
        left("d1", m, a2_like)

    loop(1, n, along_z)
    loop(1, n, along_y)
    loop(0, n, across)
    loop(0, 2 * n, cores)
    for i in range(1, 4):
        left("wc", lax.rem(spot + i, 4), wc.at[spot])
    for out in outs:
        out.wait()


def on_device(feats, weight, weight_mask, tile_vals, edge_mask, tile_pos, grad_out):
    reps = lax.axis_size("rep")
    n = reps // 2
    block, width = feats.shape
    tiles, side, _ = tile_vals.shape
    rows = block // (4 * n)
    share = width // reps
    places, total = semaphore_places(n)
    chunked = (reps, 2 * rows, width)
    piece = (2, rows, width)

    def vm(shape, kind=BF):
        return pltpu.VMEM(shape, kind)

    scratch = [
        vm(chunked), vm((block // side, side, width)), vm((width, width)), vm((width, width), jnp.int32),
        vm((tiles, side, side)), vm((tiles, side, side), F32),
        vm((width, width)), vm(piece), vm((4 * n,) + piece),
        vm((tiles, side, side)), vm((tiles, side, side)),
        vm((tiles, side, width)), vm((tiles, side, width)),
        vm((2 * side, tiles * side)), vm((4 * n,) + piece),
        vm((2 * n,) + piece), vm((n,) + piece), vm((n,) + piece), vm((n,) + piece), vm((n,) + piece),
        vm(piece, F32), vm(piece), vm((reps,) + piece),
        vm(chunked), vm((n,) + chunked[1:]), vm((n,) + chunked[1:]), vm((n,) + chunked[1:]),
        vm(chunked[1:], F32), vm(chunked),
        vm((width, block)), vm((reps, share, width), F32), vm((n, share, width), F32),
        vm((4, share, width), F32), vm((reps, share, width), F32), vm((width, width), F32),
        vm((tiles, side, side), F32), vm((block, width)),
        pltpu.SemaphoreType.DMA((total,)), pltpu.SemaphoreType.DMA((total,)),
        pltpu.SemaphoreType.DMA((6,)),
    ]
    anywhere = pl.BlockSpec(memory_space=pl.ANY)
    out, fgrad, wgrad, edge = pl.pallas_call(
        functools.partial(kernel, n, places),
        out_shape=(
            jax.ShapeDtypeStruct(chunked, BF),
            jax.ShapeDtypeStruct((block, width), BF),
            jax.ShapeDtypeStruct((width, width), F32),
            jax.ShapeDtypeStruct((tiles, side, side), F32),
        ),
        in_specs=[pl.BlockSpec(memory_space=pltpu.SMEM)] + [anywhere] * 6,
        out_specs=(anywhere,) * 4,
        scratch_shapes=scratch,
        compiler_params=pltpu.CompilerParams(
            collective_id=0, has_side_effects=True, vmem_limit_bytes=40 * 1024 * 1024
        ),
        cost_estimate=pl.CostEstimate(
            flops=3_000_000_000, bytes_accessed=5_000_000, transcendentals=0
        ),
        name="layer",
    )(
        tile_pos,
        feats.reshape(chunked),
        grad_out.reshape(block // side, side, width),
        weight,
        weight_mask,
        tile_vals,
        edge_mask,
    )
    return out.reshape(block, width), fgrad, wgrad, edge


def solution(mesh):
    placed = (
        P("row", None),
        P(),
        P(),
        P(("row", "rep"), None, None),
        P(("row", "rep"), None, None),
        P(("row", "rep")),
        P("row", None),
    )
    return jax.shard_map(
        on_device,
        mesh=mesh,
        in_specs=placed,
        out_specs=(P("row", None), P("row", None), P(), P(("row", "rep"), None, None)),
        check_vma=False,
    )
```

time: 877 us -> 99.8 us (0.11)
  waiting for transfers between devices: 622 us -> 0 us
  blocking collectives: 211 us -> 0 us
  Pallas kernels: 0 us -> 87.9 us
  between operations: 14 us -> 0.66 us
  matrix products: 10.1 us -> 0 us
    psum x3 -> x0, waiting for transfers between devices: 622 us -> none  [the longest x2 384 us: spread(): return lax.psum(block, axis)]
    psum x2 -> x0, blocking collectives: 211 us -> none  [the longest x1 134 us: on_device(): summed = lax.psum(col_terms[section], 'row').astype(jnp.bfloat16)]
    pallas_call x0 -> x1, Pallas kernels: none -> 87.9 us  [on_device(): pl.pallas_call(functools.partial(kernel, n, places), out_shape=(jax.Shape...]
    dot_general x8 -> x0, matrix products: 10.1 us -> none  [the longest x1 2.08 us: on_device(): lax.dot_general(feats, grad_cols, (((0,), (0,)), ((), ())), preferred_ele...]
  transfers between devices with their start and end apart: 3 -> 0, of which waited for: 3 -> 0; matrix products, arithmetic and copies ran while one was open for 0% -> 0% of each run, Pallas kernels for 0% -> 0%
where the time goes in v1:
time: 99.8 us; the launch traced here: 98.4 us
  Pallas kernels  87.9 us (88%)
  local copies, waits for them, and re-layouts  9.88 us (10%)
    pallas_call x1, Pallas kernels, on_device(): pl.pallas_call(functools.partial(kernel, n, places), out_shape=(jax.Shape...  87.9 us
    unnamed x18, local copies, waits for them, and re-layouts  9.88 us

profile of v1, /device:TPU:1, one launch (start us, length us, event | category | flops | bytes accessed | tf_op | source)
XLA Modules:
  0.0 98.4 jit_solution(6596391588584660655)
XLA Ops:
  0.6 0.0 copy-start.6
  0.6 0.6 copy-done.6
  1.3 0.0 copy-start
  1.3 1.1 %copy-done = f32[12,128,128]{2,1,0:T(8,128)S(1)} copy-done((f32[12,128,128]{2,1,0:T(8,128)S(1)}, f32[12,128,128]{2,1,0:T(8,128)}, u32[]{:S(2)}) %copy-start) | copy-done | bytes 786456
  2.4 0.0 copy-start.1
  2.4 1.0 %copy-done.1 = bf16[1024,256]{1,0:T(8,128)(2,1)S(1)} copy-done((bf16[1024,256]{1,0:T(8,128)(2,1)S(1)}, bf16[1024,256]{1,0:T(8,128)(2,1)}, u32[]{:S(2)}) %copy-start.1) | copy-done | bytes 524312
  3.5 0.0 copy-start.2
  3.5 1.0 %copy-done.2 = bf16[1024,256]{1,0:T(8,128)(2,1)S(1)} copy-done((bf16[1024,256]{1,0:T(8,128)(2,1)S(1)}, bf16[1024,256]{1,0:T(8,128)(2,1)}, u32[]{:S(2)}) %copy-start.2) | copy-done | bytes 524312
  4.5 0.0 copy-start.3
  4.5 1.0 %copy-done.3 = bf16[12,128,128]{2,1,0:T(8,128)(2,1)S(1)} copy-done((bf16[12,128,128]{2,1,0:T(8,128)(2,1)S(1)}, bf16[12,128,128]{2,1,0:T(8,128)(2,1)}, u32[]{:S(2)}) %copy-start.3) | copy-done | bytes 393240
  5.5 0.0 copy-start.4
  5.5 0.9 copy-done.4
  6.5 0.0 copy-start.5
  6.5 0.9 copy-done.5
  7.4 87.9 %layer.1 = (bf16[16,64,256]{2,1,0:T(8,128)(2,1)S(1)}, bf16[1024,256]{1,0:T(8,128)(2,1)S(1)}, f32[256,256]{1,0:T(8,128)S(1)}, f32[12,128,128]{2,1,0:T(8,128)S(1)}) custom-call(s32[12]{0:T(128)S(1)} %copy-done.6, bf16[16,64,256]{2,1,0:T(8,128)(2,1)S(1)} %bitcast.4, bf16[8,128,256]{2,1,0:T(8,128)(2,1)S(1)} %bitcast.5, bf16[256,256]{1,0:T(8,128)(2,1)S(1)} %copy-done.5, ...), custom_call_target="tpu_custom_call" | custom-call | flops 3000000000 | bytes 5000000 | tf_op jit(solution)/shard_map/layer/pallas_call | solution.py:470
  95.3 0.8 copy.15
  96.1 0.8 copy.16
  96.9 0.7 copy.17
  97.6 0.9 copy.18
Async XLA Ops:
  0.6 0.7 copy-start.6
  1.3 1.1 %copy-start = (f32[12,128,128]{2,1,0:T(8,128)S(1)}, f32[12,128,128]{2,1,0:T(8,128)}, u32[]{:S(2)}) copy-start(f32[12,128,128]{2,1,0:T(8,128)} %em_h.1) | copy-start | bytes 2359300
  2.4 1.0 %copy-start.1 = (bf16[1024,256]{1,0:T(8,128)(2,1)S(1)}, bf16[1024,256]{1,0:T(8,128)(2,1)}, u32[]{:S(2)}) copy-start(bf16[1024,256]{1,0:T(8,128)(2,1)} %param.7) | copy-start | bytes 1572868
  3.5 1.0 %copy-start.2 = (bf16[1024,256]{1,0:T(8,128)(2,1)S(1)}, bf16[1024,256]{1,0:T(8,128)(2,1)}, u32[]{:S(2)}) copy-start(bf16[1024,256]{1,0:T(8,128)(2,1)} %param.13) | copy-start | bytes 1572868
  4.5 1.0 %copy-start.3 = (bf16[12,128,128]{2,1,0:T(8,128)(2,1)S(1)}, bf16[12,128,128]{2,1,0:T(8,128)(2,1)}, u32[]{:S(2)}) copy-start(bf16[12,128,128]{2,1,0:T(8,128)(2,1)} %tv_h.1) | copy-start | bytes 1179652
  5.5 0.9 copy-start.4
  6.5 0.9 copy-start.5

commit v2 on v1

v2 whole, which is shorter than its diff:
```python
import functools

import jax
import jax.numpy as jnp
from jax import lax
from jax.experimental import pallas as pl
from jax.experimental.pallas import tpu as pltpu
from jax.sharding import PartitionSpec as P

BF = jnp.bfloat16
F32 = jnp.float32
VMEM_MIB = 56


def semaphore_places(n):
    counts = dict(
        a1=n, a3=n, a4=2 * n,
        d1=n, d2=n // 2, d3=n, d5=n, d6=n,
        c1=n, c2=n, c3=n, c4=n,
        wx=8, wz=n, wy=n, wa=n, wb=8,
    )
    places, total = {}, 0
    for name, count in counts.items():
        places[name] = total
        total += count
    return places, total


def loop(low, high, step):
    def run(i, carry):
        step(i)
        return carry

    lax.fori_loop(low, high, run, 0)


def kernel(
    n, places,
    pos_ref, feats_h, gout_h, w_h, wm_h, tv_h, em_h,
    out_h, fg_h, wg_h, ge_h,
    chunk, gout, w, wm, tv, em,
    weff, pj, mk, mkt, gs, rsf, rs, lhs, pb,
    d1r, d2s, d2r, d3s, d3r, gc,
    yb, c1r, c2s, c2r, c2o, oc,
    wl, wxs, wxr, wzs, wzr, wyr, wag, wgo, ge, fg,
    send, recv, local,
):
    row, rep = lax.axis_index("row"), lax.axis_index("rep")
    z, xl, c = row // 4, row // 2 % 2, row % 2
    xh, y = rep // n, rep % n
    reps = 2 * n
    half = n // 2
    tiles, side, _ = tv.shape
    width = w.shape[0]
    chunk_rows = chunk.shape[0]
    per_side = gout.shape[0]
    cpt = side // chunk_rows
    block = per_side * side
    spot = xh * 4 + xl * 2 + c

    def row_of(zz, xx, cc):
        return zz * 4 + xx * 2 + cc

    core_row, lo_row = row_of(z, xl, 1 - c), row_of(z, 1 - xl, c)
    hi_rep = (1 - xh) * n + y
    quarter = (c * 2 + xl) * half
    section, group = row // reps, lax.rem(row, reps)

    def around(at, o):
        return lax.rem(at + o, n)

    def copy(name, i, j, src, dst, to_row, to_rep):
        return pltpu.make_async_remote_copy(
            src_ref=src,
            dst_ref=dst,
            send_sem=send.at[places[name] + i],
            recv_sem=recv.at[places[name] + j],
            device_id=(to_row, to_rep),
            device_id_type=pl.DeviceIdType.MESH,
        )

    def arrived(name, j, ref):
        copy(name, 0, j, ref, ref, core_row, rep).wait_recv()

    def left(name, i, ref):
        copy(name, i, 0, ref, ref, core_row, rep).wait_send()

    def owner(k, i):
        return k * reps + rep, quarter + i

    def reader(zz):
        return row_of(zz, y // half, xh), group

    def line(s):
        return row_of(z, lax.rem(s // 2, 2), lax.rem(s, 2)), s // 4 * n + y

    def is_me(r, q):
        return jnp.logical_and(r == row, q == rep)

    def send_or_keep(name, i, j, src, dst, r, q):
        same = is_me(r, q)

        @pl.when(jnp.logical_not(same))
        def _():
            copy(name, i, j, src, dst, r, q).start()

        @pl.when(same)
        def _():
            pltpu.make_async_copy(src, dst, recv.at[places[name] + j]).start()

    ins = []
    for i, (src, dst) in enumerate(
        ((feats_h.at[rep], chunk), (tv_h, tv), (em_h, em), (gout_h, gout), (w_h, w), (wm_h, wm))
    ):
        ins.append(pltpu.make_async_copy(src, dst, local.at[i]))
        ins[-1].start()

    barrier = pltpu.get_barrier_semaphore()

    def greet(r, q):
        pl.semaphore_signal(barrier, inc=1, device_id=(r, q), device_id_type=pl.DeviceIdType.MESH)

    def greet_other(r, q):
        pl.when(jnp.logical_not(is_me(r, q)))(functools.partial(greet, r, q))

    loop(0, n, lambda i: greet_other(*reader(i)))
    loop(0, n, lambda m: greet_other(*owner(m // half, lax.rem(m, half))))
    loop(1, 8, lambda o: greet(*line(lax.rem(spot + o, 8))))
    loop(1, n, lambda o: greet(row_of(around(z, o), xl, c), rep))
    loop(1, n, lambda o: greet(row, xh * n + around(y, o)))
    same = jnp.logical_and(group == rep, jnp.logical_and(y // half == xl, xh == c))
    expected = 7 + 2 * (n - 1) + 2 * n - 2 * same.astype(jnp.int32)

    ins[0].wait()
    pl.semaphore_wait(barrier, expected)

    def a1_step(o):
        zz = around(z, o)
        r, q = reader(zz)
        send_or_keep("a1", zz, section * half + lax.rem(rep, half), chunk, pj.at[rep, section], r, q)

    loop(0, n, a1_step)

    picks = []
    for t in range(tiles):
        pos = pos_ref[t]
        slot = jnp.maximum(pos, 0)
        picks.append(
            (
                pos >= 0,
                lax.rem(slot // per_side, per_side),
                slot // (per_side * per_side),
                lax.rem(slot, per_side),
            )
        )

    ins[1].wait()
    ins[2].wait()
    ins[3].wait()
    for t in range(tiles):
        product = tv[t].astype(F32) * em[t]
        mk[t] = product.astype(BF)
        mkt[t] = product.T.astype(BF)
        gs[t] = gout[picks[t][1]]

    def chosen(cond, tile):
        return lax.select_n(cond, jnp.zeros_like(tile), tile)

    def backward_tile(jj):
        for k in range(2):
            for t in range(tiles):
                live, _, kt, jt = picks[t]
                cond = jnp.logical_and(live, jnp.logical_and(kt == k, jt == jj))
                lhs[k * side:(k + 1) * side, t * side:(t + 1) * side] = chosen(cond, mkt[t])
        total = jnp.dot(lhs[...], gs[...].reshape(tiles * side, width), preferred_element_type=F32)
        total = total.astype(BF)
        for k in range(2):
            pb[pl.ds(jj * cpt, cpt), k] = total[k * side:(k + 1) * side].reshape(cpt, chunk_rows, width)

    quarter_tiles = half // cpt

    def send_quarter(x):
        def one(i):
            m = x * half + i
            copy("d1", m, m, pb.at[(1 - c) * n + m], d1r.at[m], core_row, rep).start()

        first = ((1 - c) * 2 + x) * quarter_tiles
        loop(0, quarter_tiles, lambda i: backward_tile(first + i))
        loop(0, half, one)

    send_quarter(1 - xl)
    send_quarter(xl)
    loop(0, 2 * quarter_tiles, lambda i: backward_tile(c * 2 * quarter_tiles + i))

    def d2_step(o):
        i = lax.rem(z + o, half)
        m = (1 - xl) * half + i
        arrived("d1", m, d1r.at[m])
        d2s[i] = (pb[c * n + m].astype(F32) + d1r[m].astype(F32)).astype(BF)
        copy("d2", i, i, d2s.at[i], d2r.at[i], lo_row, rep).start()

    loop(0, half, d2_step)

    def chunk_of(x, m):
        return pj.at[(c * 2 + x) * half + lax.rem(m, half), m // half]

    def pass_core(x, m):
        ref = chunk_of(x, m)
        copy("a4", x * n + m, x * n + m, ref, ref, core_row, rep).start()

    def a1_arrival(m):
        ref = chunk_of(xl, m)
        arrived("a1", m, chunk)
        copy("a3", m, m, ref, ref, lo_row, rep).start()
        pass_core(xl, m)

    loop(0, n, a1_arrival)

    def d3_step(o):
        i = lax.rem(z + o, half)
        m = xl * half + i
        arrived("d1", m, d1r.at[m])
        arrived("d2", i, d2r.at[i])
        total = pb[c * n + m].astype(F32) + d1r[m].astype(F32) + d2r[i].astype(F32)
        d3s[i] = total.astype(BF)
        for k in range(2):
            r, q = owner(k, i)
            send_or_keep("d3", k * half + i, z, d3s.at[i, k], d3r.at[z], r, q)

    loop(0, half, d3_step)

    def a3_arrival(m):
        arrived("a3", m, chunk)
        pass_core(1 - xl, m)

    loop(0, n, a3_arrival)
    ins[4].wait()
    ins[5].wait()
    weff[...] = jnp.where(wm[...] != 0, w[...].astype(F32), 0.0).astype(BF)
    loop(0, 2 * n, lambda m: arrived("a4", m, chunk))

    for t in range(tiles):
        _, _, kt, jt = picks[t]
        rsf[t] = pj[pl.ds(jt * cpt, cpt), kt].reshape(side, width)
    rs[...] = (
        jnp.dot(rsf[...].reshape(tiles * side, width), weff[...], preferred_element_type=F32)
        .astype(BF)
        .reshape(tiles, side, width)
    )

    chunks_pair = 2 * side // chunk_rows
    pairs_half = block // 2 // (2 * side)

    def forward_pair(u):
        for h in range(2):
            for t in range(tiles):
                live, it, _, _ = picks[t]
                cond = jnp.logical_and(live, it == 2 * u + h)
                lhs[h * side:(h + 1) * side, t * side:(t + 1) * side] = chosen(cond, mk[t])
        total = jnp.dot(lhs[...], rs[...].reshape(tiles * side, width), preferred_element_type=F32)
        yb[pl.ds(u * chunks_pair, chunks_pair)] = total.astype(BF).reshape(
            chunks_pair, chunk_rows, width
        )

    loop(0, pairs_half, lambda i: forward_pair((1 - xh) * pairs_half + i))

    def c1_step(o):
        yy = around(y, o)
        copy("c1", yy, yy, yb.at[(1 - xh) * n + yy], c1r.at[yy], row, hi_rep).start()

    loop(1, n + 1, c1_step)

    wl[...] = jnp.zeros_like(wl)
    deep = max(1, 256 // (2 * chunk_rows))

    def weight_step(i):
        at = pl.ds(i * deep, deep)
        left_side = pj[at].reshape(2 * deep * chunk_rows, width)
        right_side = pb[at].reshape(2 * deep * chunk_rows, width)
        wl[...] += lax.dot_general(
            left_side, right_side, (((0,), (0,)), ((), ())), preferred_element_type=F32
        ).reshape(wl.shape)

    loop(0, reps // deep, weight_step)
    wxs[...] = wl[...].astype(BF)

    def wx_step(o):
        s = lax.rem(spot + o, 8)
        r, q = line(s)
        copy("wx", s, spot, wxs.at[s], wxr.at[spot], r, q).start()

    loop(1, 8, wx_step)
    loop(0, pairs_half, lambda i: forward_pair(xh * pairs_half + i))

    def pass_hi(name, ref, yy):
        at = xh * n + yy
        copy(name, yy, yy, ref.at[at], ref.at[at], row, hi_rep).start()

    def pass_y(name, ref, o):
        yy = around(y, o)
        copy(name, yy, y, ref.at[rep], ref.at[rep], row, xh * n + yy).start()

    loop(0, n, lambda i: arrived("d3", i, chunk))
    gc[rep] = functools.reduce(jnp.add, [d3r[i].astype(F32) for i in range(n)]).astype(BF)
    pass_hi("d6", gc, y)
    loop(1, n, lambda o: pass_y("d5", gc, o))

    def c2_sum(yy):
        arrived("c1", yy, chunk)
        return yb[xh * n + yy].astype(F32) + c1r[yy].astype(F32)

    def c2_step(o):
        yy = around(y, o)
        c2s[yy] = c2_sum(yy).astype(BF)
        copy("c2", yy, y, c2s.at[yy], c2r.at[y], row, xh * n + yy).start()

    loop(1, n, c2_step)
    c2o[...] = c2_sum(y)

    share = wl.shape[1]
    tall = share * 2 // n

    def wx_arrival(o):
        s = lax.rem(spot + o, 8)
        arrived("wx", s, wxr.at[s])
        wl[spot] += wxr[s].astype(F32)

    loop(1, 8, wx_arrival)
    mine = wl[spot]
    for i in range(n):
        g, h = i // 2, i % 2
        wzs[i] = mine[g * tall:(g + 1) * tall, h * 128:(h + 1) * 128]

    def wz_step(o):
        zz = around(z, o)
        copy("wz", zz, z, wzs.at[zz], wzr.at[z], row_of(zz, xl, c), rep).start()

    loop(1, n, wz_step)

    def relay(got, gone, ref, o):
        yy = around(y, o)
        arrived(got, yy, chunk)
        pass_hi(gone, ref, yy)

    loop(1, n, lambda o: relay("d5", "d6", gc, o))

    def c2_add(o):
        yy = around(y, o)
        arrived("c2", yy, chunk)
        c2o[...] += c2r[yy].astype(F32)

    loop(1, n, c2_add)
    oc[rep] = c2o[...].astype(BF)
    pass_hi("c4", oc, y)
    loop(1, n, lambda o: pass_y("c3", oc, o))

    def wz_arrival(o):
        zz = around(z, o)
        arrived("wz", zz, wzr.at[zz])
        wzs[z] += wzr[zz]

    loop(1, n, wz_arrival)
    wyr[y] = wzs[z]

    def wy_step(o):
        yy = around(y, o)
        copy("wy", yy, y, wyr.at[y], wyr.at[y], row, xh * n + yy).start()

    loop(1, n, wy_step)

    for t in range(tiles):
        live = picks[t][0]
        scores = lax.dot_general(gs[t], rs[t], (((1,), (1,)), ((), ())), preferred_element_type=F32)
        ge[t] = chosen(live, tv[t].astype(F32) * scores)
    outs = [pltpu.make_async_copy(ge, ge_h, local.at[0])]
    outs[-1].start()

    loop(1, n, lambda o: arrived("wy", around(y, o), wyr.at[y]))
    wag[spot, z] = functools.reduce(jnp.add, [wyr[i] for i in range(n)])

    def wa_step(o):
        zz = around(z, o)
        copy("wa", zz, z, wag.at[spot, z], wag.at[spot, z], row_of(zz, xl, c), rep).start()

    loop(1, n, wa_step)
    loop(1, n, lambda o: relay("c3", "c4", oc, o))

    loop(0, n, lambda yy: arrived("d6", yy, chunk))
    fg[...] = lax.dot_general(
        gc[...].reshape(block, width), weff[...], (((1,), (1,)), ((), ())), preferred_element_type=F32
    ).astype(BF)
    outs.append(pltpu.make_async_copy(fg, fg_h, local.at[1]))
    outs[-1].start()

    loop(1, n, lambda o: arrived("wa", around(z, o), wyr.at[y]))

    def wb_step(o):
        s = lax.rem(spot + o, 8)
        r, q = line(s)
        copy("wb", s, spot, wag.at[spot], wag.at[spot], r, q).start()

    loop(1, 8, wb_step)

    loop(0, n, lambda yy: arrived("c4", yy, chunk))
    outs.append(pltpu.make_async_copy(oc, out_h, local.at[2]))
    outs[-1].start()

    loop(1, 8, lambda o: arrived("wb", lax.rem(spot + o, 8), wag.at[spot]))
    for s in range(8):
        for i in range(n):
            g, h = i // 2, i % 2
            top = s * share + g * tall
            at = (slice(top, top + tall), slice(h * 128, (h + 1) * 128))
            wgo[at] = jnp.where(wm[at] != 0, wag[s, i], 0.0)
    outs.append(pltpu.make_async_copy(wgo, wg_h, local.at[3]))
    outs[-1].start()

    def left_if_sent(name, i, r, q):
        pl.when(jnp.logical_not(is_me(r, q)))(functools.partial(left, name, i, chunk))

    loop(0, n, lambda i: left_if_sent("a1", i, *reader(i)))
    loop(0, n, lambda m: left_if_sent("d3", m, *owner(m // half, lax.rem(m, half))))

    def along(o):
        zz, yy = around(z, o), around(y, o)
        left("wz", zz, wyr.at[y])
        left("wa", zz, wyr.at[y])
        left("wy", yy, wyr.at[y])
        left("d5", yy, chunk)
        left("c2", yy, chunk)
        left("c3", yy, chunk)

    def across(i):
        left("a3", i, chunk)
        left("d1", i, d1r.at[0])
        left("d6", i, chunk)
        left("c1", i, chunk)
        left("c4", i, chunk)
        left("a4", i, chunk)
        left("a4", n + i, chunk)

    def over_line(o):
        s = lax.rem(spot + o, 8)
        left("wx", s, wxs.at[s])
        left("wb", s, wag.at[spot])

    loop(1, n, along)
    loop(0, n, across)
    loop(0, half, lambda i: left("d2", i, d1r.at[0]))
    loop(1, 8, over_line)
    for out in outs:
        out.wait()


def settle_kernel(*refs):
    pairs, sem = list(zip(refs[:4], refs[4:8])), refs[8]
    copies = [pltpu.make_async_copy(src, dst, sem.at[i]) for i, (src, dst) in enumerate(pairs)]
    for one in copies:
        one.start()
    for one in copies:
        one.wait()


def settle(*arrays):
    anywhere = pl.BlockSpec(memory_space=pl.ANY)
    return pl.pallas_call(
        settle_kernel,
        out_shape=tuple(jax.ShapeDtypeStruct(a.shape, a.dtype) for a in arrays),
        in_specs=[anywhere] * 4,
        out_specs=(anywhere,) * 4,
        scratch_shapes=[pltpu.SemaphoreType.DMA((4,))],
        compiler_params=pltpu.CompilerParams(vmem_limit_bytes=VMEM_MIB * 1024 * 1024),
        name="settle",
    )(*arrays)


def on_device(feats, weight, weight_mask, tile_vals, edge_mask, tile_pos, grad_out):
    reps = lax.axis_size("rep")
    n = reps // 2
    block, width = feats.shape
    tiles, side, _ = tile_vals.shape
    rows = block // reps
    share = width // 8
    tall = share * 2 // n
    places, total = semaphore_places(n)
    chunked = (reps, rows, width)
    pair = (2, rows, width)

    def vm(shape, kind=BF):
        return pltpu.VMEM(shape, kind)

    scratch = [
        vm(chunked[1:]), vm((block // side, side, width)), vm((width, width)), vm((width, width), jnp.int32),
        vm((tiles, side, side)), vm((tiles, side, side), F32),
        vm((width, width)), vm((reps,) + pair),
        vm((tiles, side, side)), vm((tiles, side, side)),
        vm((tiles, side, width)), vm((tiles, side, width)), vm((tiles, side, width)),
        vm((2 * side, tiles * side)), vm((reps,) + pair),
        vm((n,) + pair), vm((n // 2,) + pair), vm((n // 2,) + pair), vm((n // 2,) + pair),
        vm((n,) + chunked[1:]), vm(chunked),
        vm(chunked), vm((n,) + chunked[1:]), vm((n,) + chunked[1:]), vm((n,) + chunked[1:]),
        vm(chunked[1:], F32), vm(chunked),
        vm((8, share, width), F32), vm((8, share, width)), vm((8, share, width)),
        vm((n, tall, 128), F32), vm((n, tall, 128), F32), vm((n, tall, 128), F32),
        vm((8, n, tall, 128), F32), vm((width, width), F32),
        vm((tiles, side, side), F32), vm((block, width)),
        pltpu.SemaphoreType.DMA((total,)), pltpu.SemaphoreType.DMA((total,)),
        pltpu.SemaphoreType.DMA((6,)),
    ]
    anywhere = pl.BlockSpec(memory_space=pl.ANY)
    out, fgrad, wgrad, edge = pl.pallas_call(
        functools.partial(kernel, n, places),
        out_shape=(
            jax.ShapeDtypeStruct(chunked, BF),
            jax.ShapeDtypeStruct((block, width), BF),
            jax.ShapeDtypeStruct((width, width), F32),
            jax.ShapeDtypeStruct((tiles, side, side), F32),
        ),
        in_specs=[pl.BlockSpec(memory_space=pltpu.SMEM)] + [anywhere] * 6,
        out_specs=(anywhere,) * 4,
        scratch_shapes=scratch,
        compiler_params=pltpu.CompilerParams(
            collective_id=0, has_side_effects=True, vmem_limit_bytes=VMEM_MIB * 1024 * 1024
        ),
        cost_estimate=pl.CostEstimate(
            flops=3_000_000_000, bytes_accessed=5_000_000, transcendentals=0
        ),
        name="layer",
    )(
        tile_pos,
        feats.reshape(chunked),
        grad_out.reshape(block // side, side, width),
        weight,
        weight_mask,
        tile_vals,
        edge_mask,
    )
    return settle(out.reshape(block, width), fgrad, wgrad, edge)


def solution(mesh):
    placed = (
        P("row", None),
        P(),
        P(),
        P(("row", "rep"), None, None),
        P(("row", "rep"), None, None),
        P(("row", "rep")),
        P("row", None),
    )
    return jax.shard_map(
        on_device,
        mesh=mesh,
        in_specs=placed,
        out_specs=(P("row", None), P("row", None), P(), P(("row", "rep"), None, None)),
        check_vma=False,
    )
```

time: 99.8 us -> 161 us (1.61)
  Pallas kernels: 87.9 us -> 160 us
  local copies, waits for them, and re-layouts: 9.88 us -> 0 us
    pallas_call x0 -> x1, Pallas kernels: none -> 64.7 us  [settle(): pl.pallas_call(settle_kernel, out_shape=tuple((jax.ShapeDtypeStruct(a.sha...]
    unnamed x18 -> x0, local copies, waits for them, and re-layouts: 9.88 us -> none
    pallas_call x1, Pallas kernels: 87.9 us -> 95.8 us  [on_device(): pl.pallas_call(functools.partial(kernel, n, places), out_shape=(jax.Shape...]
where the time goes in v2:
time: 161 us
  Pallas kernels  160 us (99%)
    pallas_call x1, Pallas kernels, on_device(): pl.pallas_call(functools.partial(kernel, n, places), out_shape=(jax.Shape...  95.8 us
    pallas_call x1, Pallas kernels, settle(): pl.pallas_call(settle_kernel, out_shape=tuple((jax.ShapeDtypeStruct(a.sha...  64.7 us

profile of v2, /device:TPU:1, one launch (start us, length us, event | category | flops | bytes accessed | tf_op | source)
XLA Modules:
  0.0 161.1 jit_solution(1026244778282018969)
XLA Ops:
  0.6 95.8 %layer.1 = (bf16[16,64,256]{2,1,0:T(8,128)(2,1)}, bf16[1024,256]{1,0:T(8,128)(2,1)}, f32[256,256]{1,0:T(8,128)}, f32[12,128,128]{2,1,0:T(8,128)}) custom-call(s32[12]{0:T(128)} %pos_ref.1, bf16[16,64,256]{2,1,0:T(8,128)(2,1)} %bitcast.4, bf16[8,128,256]{2,1,0:T(8,128)(2,1)} %bitcast.5, bf16[256,256]{1,0:T(8,128)(2,1)} %w_h.1, s32[256,256]{1,0:T(8,128)} %wm_h.1, ...), custom_call_target="tpu_custom_call" | custom-call | flops 3000000000 | bytes 5000000 | tf_op jit(solution)/shard_map/layer/pallas_call | solution.py:511
  96.5 64.7 %settle.1 = (bf16[1024,256]{1,0:T(8,128)(2,1)}, bf16[1024,256]{1,0:T(8,128)(2,1)}, f32[256,256]{1,0:T(8,128)}, f32[12,128,128]{2,1,0:T(8,128)}) custom-call(bf16[1024,256]{1,0:T(8,128)(2,1)} %bitcast.3, bf16[1024,256]{1,0:T(8,128)(2,1)} %get-tuple-element.9.refs_1_, f32[256,256]{1,0:T(8,128)} %get-tuple-element.10.refs_2_, ...), custom_call_target="tpu_custom_call" | custom-call | tf_op jit(solution)/shard_map/settle/pallas_call | solution.py:466

commit v3 on v2

--- a/solution.py
+++ b/solution.py
@@ -12,12 +12,16 @@
 VMEM_MIB = 56
 
 
+def doublings(n):
+    return n.bit_length() - 1
+
+
 def semaphore_places(n):
     counts = dict(
         a1=n, a3=n, a4=2 * n,
         d1=n, d2=n // 2, d3=n, d5=n, d6=n,
         c1=n, c2=n, c3=n, c4=n,
-        wx=8, wz=n, wy=n, wa=n, wb=8,
+        w5=2 + doublings(n),
     )
     places, total = {}, 0
     for name, count in counts.items():
@@ -42,8 +46,8 @@
     weff, pj, mk, mkt, gs, rsf, rs, lhs, pb,
     d1r, d2s, d2r, d3s, d3r, gc,
     yb, c1r, c2s, c2r, c2o, oc,
-    wl, wxs, wxr, wzs, wzr, wyr, wag, wgo, ge, fg,
-    send, recv, local,
+    wl, w5s, w5r, wgo, ge, fg,
+    send, recv, local, round_y, round_x,
 ):
     row, rep = lax.axis_index("row"), lax.axis_index("rep")
     z, xl, c = row // 4, row // 2 % 2, row % 2
@@ -120,19 +124,30 @@
     def greet(r, q):
         pl.semaphore_signal(barrier, inc=1, device_id=(r, q), device_id_type=pl.DeviceIdType.MESH)
 
-    def greet_other(r, q):
-        pl.when(jnp.logical_not(is_me(r, q)))(functools.partial(greet, r, q))
-
-    loop(0, n, lambda i: greet_other(*reader(i)))
-    loop(0, n, lambda m: greet_other(*owner(m // half, lax.rem(m, half))))
-    loop(1, 8, lambda o: greet(*line(lax.rem(spot + o, 8))))
+    def greet_line(sem):
+        def one(o):
+            r, q = line(lax.rem(spot + o, 8))
+            pl.semaphore_signal(sem, inc=1, device_id=(r, q), device_id_type=pl.DeviceIdType.MESH)
+
+        loop(1, 8, one)
+
+    def greet_y(sem):
+        def one(o):
+            q = xh * n + around(y, o)
+            pl.semaphore_signal(sem, inc=1, device_id=(row, q), device_id_type=pl.DeviceIdType.MESH)
+
+        loop(1, n, one)
+
     loop(1, n, lambda o: greet(row_of(around(z, o), xl, c), rep))
-    loop(1, n, lambda o: greet(row, xh * n + around(y, o)))
-    same = jnp.logical_and(group == rep, jnp.logical_and(y // half == xl, xh == c))
-    expected = 7 + 2 * (n - 1) + 2 * n - 2 * same.astype(jnp.int32)
+    greet_y(barrier)
+    greet_line(barrier)
+    pl.semaphore_wait(barrier, 7 + 2 * (n - 1))
+    greet_y(round_y)
+    pl.semaphore_wait(round_y, n - 1)
+    greet_line(round_x)
+    pl.semaphore_wait(round_x, 7)
 
     ins[0].wait()
-    pl.semaphore_wait(barrier, expected)
 
     def a1_step(o):
         zz = around(z, o)
@@ -258,17 +273,9 @@
                 cond = jnp.logical_and(live, it == 2 * u + h)
                 lhs[h * side:(h + 1) * side, t * side:(t + 1) * side] = chosen(cond, mk[t])
         total = jnp.dot(lhs[...], rs[...].reshape(tiles * side, width), preferred_element_type=F32)
-        yb[pl.ds(u * chunks_pair, chunks_pair)] = total.astype(BF).reshape(
+        yb[pl.ds(u * chunks_pair, chunks_pair), 0:chunk_rows] = total.astype(BF).reshape(
             chunks_pair, chunk_rows, width
         )
-
-    loop(0, pairs_half, lambda i: forward_pair((1 - xh) * pairs_half + i))
-
-    def c1_step(o):
-        yy = around(y, o)
-        copy("c1", yy, yy, yb.at[(1 - xh) * n + yy], c1r.at[yy], row, hi_rep).start()
-
-    loop(1, n + 1, c1_step)
 
     wl[...] = jnp.zeros_like(wl)
     deep = max(1, 256 // (2 * chunk_rows))
@@ -279,17 +286,19 @@
         right_side = pb[at].reshape(2 * deep * chunk_rows, width)
         wl[...] += lax.dot_general(
             left_side, right_side, (((0,), (0,)), ((), ())), preferred_element_type=F32
-        ).reshape(wl.shape)
+        )
 
     loop(0, reps // deep, weight_step)
-    wxs[...] = wl[...].astype(BF)
-
-    def wx_step(o):
-        s = lax.rem(spot + o, 8)
-        r, q = line(s)
-        copy("wx", s, spot, wxs.at[s], wxr.at[spot], r, q).start()
-
-    loop(1, 8, wx_step)
+    yb[:, chunk_rows:] = wl[...].astype(BF).reshape(reps, width // reps, width)
+
+    loop(0, pairs_half, lambda i: forward_pair((1 - xh) * pairs_half + i))
+
+    def c1_step(o):
+        yy = around(y, o)
+        copy("c1", yy, yy, yb.at[(1 - xh) * n + yy], c1r.at[yy], row, hi_rep).start()
+
+    loop(1, n + 1, c1_step)
+
     loop(0, pairs_half, lambda i: forward_pair(xh * pairs_half + i))
 
     def pass_hi(name, ref, yy):
@@ -306,7 +315,7 @@
     loop(1, n, lambda o: pass_y("d5", gc, o))
 
     def c2_sum(yy):
-        arrived("c1", yy, chunk)
+        arrived("c1", yy, c1r.at[yy])
         return yb[xh * n + yy].astype(F32) + c1r[yy].astype(F32)
 
     def c2_step(o):
@@ -317,73 +326,56 @@
     loop(1, n, c2_step)
     c2o[...] = c2_sum(y)
 
-    share = wl.shape[1]
-    tall = share * 2 // n
-
-    def wx_arrival(o):
-        s = lax.rem(spot + o, 8)
-        arrived("wx", s, wxr.at[s])
-        wl[spot] += wxr[s].astype(F32)
-
-    loop(1, 8, wx_arrival)
-    mine = wl[spot]
-    for i in range(n):
-        g, h = i // 2, i % 2
-        wzs[i] = mine[g * tall:(g + 1) * tall, h * 128:(h + 1) * 128]
-
-    def wz_step(o):
-        zz = around(z, o)
-        copy("wz", zz, z, wzs.at[zz], wzr.at[z], row_of(zz, xl, c), rep).start()
-
-    loop(1, n, wz_step)
-
     def relay(got, gone, ref, o):
         yy = around(y, o)
-        arrived(got, yy, chunk)
+        arrived(got, yy, ref.at[rep])
         pass_hi(gone, ref, yy)
 
     loop(1, n, lambda o: relay("d5", "d6", gc, o))
 
     def c2_add(o):
         yy = around(y, o)
-        arrived("c2", yy, chunk)
+        arrived("c2", yy, c2r.at[yy])
         c2o[...] += c2r[yy].astype(F32)
 
     loop(1, n, c2_add)
-    oc[rep] = c2o[...].astype(BF)
+
+    def edge_tile(t):
+        scores = lax.dot_general(gs[t], rs[t], (((1,), (1,)), ((), ())), preferred_element_type=F32)
+        ge[t] = chosen(picks[t][0], tv[t].astype(F32) * scores)
+
+    partners = [core_row, lo_row]
+    for bit in range(doublings(n)):
+        up = 1 - 2 * lax.rem(z // 2**bit, 2)
+        partners.append(row_of(z + up * 2**bit, xl, c))
+
+    def w5_send(i):
+        copy("w5", i, i, w5s.at[i], w5r.at[i], partners[i], rep).start()
+
+    def w5_step(i):
+        arrived("w5", i, w5r.at[i])
+        w5s[i + 1] = w5s[i] + w5r[i]
+
+    w5s[0] = c2o[chunk_rows:]
+    w5_send(0)
+    oc[rep, 0:chunk_rows] = c2o[0:chunk_rows].astype(BF)
+    w5_step(0)
+    w5_send(1)
+    for t in range(tiles // 2):
+        edge_tile(t)
+    w5_step(1)
+    w5_send(2)
+    for t in range(tiles // 2, tiles):
+        edge_tile(t)
+    outs = [pltpu.make_async_copy(ge, ge_h, local.at[0])]
+    outs[-1].start()
+    w5_step(2)
+    for i in range(3, len(partners)):
+        w5_send(i)
+        w5_step(i)
+    oc[rep, chunk_rows:] = w5s[len(partners)].astype(BF)
     pass_hi("c4", oc, y)
     loop(1, n, lambda o: pass_y("c3", oc, o))
-
-    def wz_arrival(o):
-        zz = around(z, o)
-        arrived("wz", zz, wzr.at[zz])
-        wzs[z] += wzr[zz]
-
-    loop(1, n, wz_arrival)
-    wyr[y] = wzs[z]
-
-    def wy_step(o):
-        yy = around(y, o)
-        copy("wy", yy, y, wyr.at[y], wyr.at[y], row, xh * n + yy).start()
-
-    loop(1, n, wy_step)
-
-    for t in range(tiles):
-        live = picks[t][0]
-        scores = lax.dot_general(gs[t], rs[t], (((1,), (1,)), ((), ())), preferred_element_type=F32)
-        ge[t] = chosen(live, tv[t].astype(F32) * scores)
-    outs = [pltpu.make_async_copy(ge, ge_h, local.at[0])]
-    outs[-1].start()
-
-    loop(1, n, lambda o: arrived("wy", around(y, o), wyr.at[y]))
-    wag[spot, z] = functools.reduce(jnp.add, [wyr[i] for i in range(n)])
-
-    def wa_step(o):
-        zz = around(z, o)
-        copy("wa", zz, z, wag.at[spot, z], wag.at[spot, z], row_of(zz, xl, c), rep).start()
-
-    loop(1, n, wa_step)
-    loop(1, n, lambda o: relay("c3", "c4", oc, o))
 
     loop(0, n, lambda yy: arrived("d6", yy, chunk))
     fg[...] = lax.dot_general(
@@ -392,26 +384,12 @@
     outs.append(pltpu.make_async_copy(fg, fg_h, local.at[1]))
     outs[-1].start()
 
-    loop(1, n, lambda o: arrived("wa", around(z, o), wyr.at[y]))
-
-    def wb_step(o):
-        s = lax.rem(spot + o, 8)
-        r, q = line(s)
-        copy("wb", s, spot, wag.at[spot], wag.at[spot], r, q).start()
-
-    loop(1, 8, wb_step)
-
-    loop(0, n, lambda yy: arrived("c4", yy, chunk))
-    outs.append(pltpu.make_async_copy(oc, out_h, local.at[2]))
+    loop(1, n, lambda o: relay("c3", "c4", oc, o))
+    loop(0, n, lambda yy: arrived("c4", yy, oc.at[rep]))
+    outs.append(pltpu.make_async_copy(oc.at[:, pl.ds(0, chunk_rows)], out_h, local.at[2]))
     outs[-1].start()
-
-    loop(1, 8, lambda o: arrived("wb", lax.rem(spot + o, 8), wag.at[spot]))
-    for s in range(8):
-        for i in range(n):
-            g, h = i // 2, i % 2
-            top = s * share + g * tall
-            at = (slice(top, top + tall), slice(h * 128, (h + 1) * 128))
-            wgo[at] = jnp.where(wm[at] != 0, wag[s, i], 0.0)
+    total = oc[:, chunk_rows:].astype(F32).reshape(width, width)
+    wgo[...] = jnp.where(wm[...] != 0, total, 0.0)
     outs.append(pltpu.make_async_copy(wgo, wg_h, local.at[3]))
     outs[-1].start()
 
@@ -422,42 +400,40 @@
     loop(0, n, lambda m: left_if_sent("d3", m, *owner(m // half, lax.rem(m, half))))
 
     def along(o):
-        zz, yy = around(z, o), around(y, o)
-        left("wz", zz, wyr.at[y])
-        left("wa", zz, wyr.at[y])
-        left("wy", yy, wyr.at[y])
+        yy = around(y, o)
         left("d5", yy, chunk)
-        left("c2", yy, chunk)
-        left("c3", yy, chunk)
+        left("c2", yy, c2s.at[yy])
+        left("c3", yy, oc.at[rep])
 
     def across(i):
         left("a3", i, chunk)
         left("d1", i, d1r.at[0])
         left("d6", i, chunk)
-        left("c1", i, chunk)
-        left("c4", i, chunk)
+        left("c1", i, c1r.at[i])
+        left("c4", i, oc.at[rep])
         left("a4", i, chunk)
         left("a4", n + i, chunk)
-
-    def over_line(o):
-        s = lax.rem(spot + o, 8)
-        left("wx", s, wxs.at[s])
-        left("wb", s, wag.at[spot])
 
     loop(1, n, along)
     loop(0, n, across)
     loop(0, half, lambda i: left("d2", i, d1r.at[0]))
-    loop(1, 8, over_line)
+    for i in range(len(partners)):
+        left("w5", i, w5s.at[i])
     for out in outs:
         out.wait()
 
 
 def settle_kernel(*refs):
-    pairs, sem = list(zip(refs[:4], refs[4:8])), refs[8]
-    copies = [pltpu.make_async_copy(src, dst, sem.at[i]) for i, (src, dst) in enumerate(pairs)]
-    for one in copies:
+    ins, outs, held = refs[:4], refs[4:8], refs[8:12]
+    sem = refs[12]
+    loads = [pltpu.make_async_copy(ins[i], held[i], sem.at[i]) for i in range(4)]
+    stores = [pltpu.make_async_copy(held[i], outs[i], sem.at[4 + i]) for i in range(4)]
+    for one in loads:
         one.start()
-    for one in copies:
+    for load, store in zip(loads, stores):
+        load.wait()
+        store.start()
+    for one in stores:
         one.wait()
 
 
@@ -468,7 +444,8 @@
         out_shape=tuple(jax.ShapeDtypeStruct(a.shape, a.dtype) for a in arrays),
         in_specs=[anywhere] * 4,
         out_specs=(anywhere,) * 4,
-        scratch_shapes=[pltpu.SemaphoreType.DMA((4,))],
+        scratch_shapes=[pltpu.VMEM(a.shape, a.dtype) for a in arrays]
+        + [pltpu.SemaphoreType.DMA((8,))],
         compiler_params=pltpu.CompilerParams(vmem_limit_bytes=VMEM_MIB * 1024 * 1024),
         name="settle",
     )(*arrays)
@@ -480,11 +457,12 @@
     block, width = feats.shape
     tiles, side, _ = tile_vals.shape
     rows = block // reps
-    share = width // 8
-    tall = share * 2 // n
+    share = width // reps
+    steps = 2 + doublings(n)
     places, total = semaphore_places(n)
     chunked = (reps, rows, width)
     pair = (2, rows, width)
+    wider = (rows + share, width)
 
     def vm(shape, kind=BF):
         return pltpu.VMEM(shape, kind)
@@ -498,14 +476,14 @@
         vm((2 * side, tiles * side)), vm((reps,) + pair),
         vm((n,) + pair), vm((n // 2,) + pair), vm((n // 2,) + pair), vm((n // 2,) + pair),
         vm((n,) + chunked[1:]), vm(chunked),
-        vm(chunked), vm((n,) + chunked[1:]), vm((n,) + chunked[1:]), vm((n,) + chunked[1:]),
-        vm(chunked[1:], F32), vm(chunked),
-        vm((8, share, width), F32), vm((8, share, width)), vm((8, share, width)),
-        vm((n, tall, 128), F32), vm((n, tall, 128), F32), vm((n, tall, 128), F32),
-        vm((8, n, tall, 128), F32), vm((width, width), F32),
+        vm((reps,) + wider), vm((n,) + wider), vm((n,) + wider), vm((n,) + wider),
+        vm(wider, F32), vm((reps,) + wider),
+        vm((width, width), F32), vm((steps + 1, share, width), F32), vm((steps, share, width), F32),
+        vm((width, width), F32),
         vm((tiles, side, side), F32), vm((block, width)),
         pltpu.SemaphoreType.DMA((total,)), pltpu.SemaphoreType.DMA((total,)),
         pltpu.SemaphoreType.DMA((6,)),
+        pltpu.SemaphoreType.REGULAR, pltpu.SemaphoreType.REGULAR,
     ]
     anywhere = pl.BlockSpec(memory_space=pl.ANY)
     out, fgrad, wgrad, edge = pl.pallas_call(

time: 161 us -> 110 us (0.68)
  the two profiles are of different devices: /device:TPU:1 before, /device:TPU:80 now
where the time goes in v3:
time: 110 us
  Pallas kernels  110 us (100%)
    pallas_call x1, Pallas kernels, on_device(): pl.pallas_call(functools.partial(kernel, n, places), out_shape=(jax.Shape...  107 us
    pallas_call x1, Pallas kernels, settle(): pl.pallas_call(settle_kernel, out_shape=tuple((jax.ShapeDtypeStruct(a.sha...  2.48 us

profile of v3, /device:TPU:80, one launch (start us, length us, event | category | flops | bytes accessed | tf_op | source)
XLA Modules:
  0.0 110.2 jit_solution(1145176310350417440)
XLA Ops:
  0.6 107.1 %layer.1 = (bf16[16,64,256]{2,1,0:T(8,128)(2,1)}, bf16[1024,256]{1,0:T(8,128)(2,1)}, f32[256,256]{1,0:T(8,128)}, f32[12,128,128]{2,1,0:T(8,128)}) custom-call(s32[12]{0:T(128)} %pos_ref.1, bf16[16,64,256]{2,1,0:T(8,128)(2,1)} %bitcast.4, bf16[8,128,256]{2,1,0:T(8,128)(2,1)} %bitcast.5, bf16[256,256]{1,0:T(8,128)(2,1)} %w_h.1, s32[256,256]{1,0:T(8,128)} %wm_h.1, ...), custom_call_target="tpu_custom_call" | custom-call | flops 3000000000 | bytes 5000000 | tf_op jit(solution)/shard_map/layer/pallas_call | solution.py:489
  107.7 2.5 %settle.1 = (bf16[1024,256]{1,0:T(8,128)(2,1)}, bf16[1024,256]{1,0:T(8,128)(2,1)}, f32[256,256]{1,0:T(8,128)}, f32[12,128,128]{2,1,0:T(8,128)}) custom-call(bf16[1024,256]{1,0:T(8,128)(2,1)} %bitcast.3, bf16[1024,256]{1,0:T(8,128)(2,1)} %get-tuple-element.9.refs_1_, f32[256,256]{1,0:T(8,128)} %get-tuple-element.10.refs_2_, ...), custom_call_target="tpu_custom_call" | custom-call | tf_op jit(solution)/shard_map/settle/pallas_call | solution.py:442

commit v4 on v1

--- a/solution.py
+++ b/solution.py
@@ -9,6 +9,7 @@
 
 BF = jnp.bfloat16
 F32 = jnp.float32
+VMEM_MIB = 56
 
 
 def semaphore_places(n):
@@ -37,11 +38,11 @@
     n, places,
     pos_ref, feats_h, gout_h, w_h, wm_h, tv_h, em_h,
     out_h, fg_h, wg_h, ge_h,
-    feats, gout, w, wm, tv, em,
-    weff, a1s, pj, mk, mkt, gs, rs, lhs, pb,
+    chunk, gout, w, wm, tv, em,
+    weff, pj, mk, mkt, gs, rsf, rs, lhs, pb,
     d1r, d2s, d2r, d3s, d3r, d3o, d4s, gc,
     yb, c1r, c2s, c2r, c2o, oc,
-    ft, wp, wz, wc, wa, wgo, ge, fg,
+    wl, wz, wc, wa, wgo, ge, fg,
     send, recv, local,
 ):
     row, rep = lax.axis_index("row"), lax.axis_index("rep")
@@ -95,7 +96,7 @@
 
     ins = []
     for i, (src, dst) in enumerate(
-        ((w_h, w), (wm_h, wm), (feats_h, feats), (tv_h, tv), (em_h, em), (gout_h, gout))
+        ((feats_h.at[rep], chunk), (tv_h, tv), (em_h, em), (gout_h, gout), (w_h, w), (wm_h, wm))
     ):
         ins.append(pltpu.make_async_copy(src, dst, local.at[i]))
         ins[-1].start()
@@ -119,16 +120,10 @@
             expected = expected + other.astype(jnp.int32)
 
     ins[0].wait()
-    ins[1].wait()
-    weff[...] = jnp.where(wm[...] != 0, w[...].astype(F32), 0.0).astype(BF)
-    ins[2].wait()
-    piece = jnp.dot(feats[rep], weff[...], preferred_element_type=F32).astype(BF)
-    a1s[...] = piece.reshape(a1s.shape)
-
     pl.semaphore_wait(barrier, expected)
 
     def scatter_piece(e):
-        src, dst = a1s.at[e], pj.at[parts[e], section]
+        src, dst = chunk.at[e], pj.at[parts[e], section]
         same = is_me(part_rows[e], group)
 
         @pl.when(jnp.logical_not(same))
@@ -155,9 +150,9 @@
             )
         )
 
+    ins[1].wait()
+    ins[2].wait()
     ins[3].wait()
-    ins[4].wait()
-    ins[5].wait()
     for t in range(tiles):
         product = tv[t].astype(F32) * em[t]
         mk[t] = product.astype(BF)
@@ -192,8 +187,8 @@
     send_quarter(1 - xl)
     send_quarter(xl)
 
-    arrived("a1", 0, a1s.at[0])
-    arrived("a1", 1, a1s.at[0])
+    arrived("a1", 0, chunk.at[0])
+    arrived("a1", 1, chunk.at[0])
 
     def pass_lo(zz):
         p = (c * 2 + xl) * n + zz
@@ -271,11 +266,34 @@
         def _(src=src, dst=dst):
             pltpu.make_async_copy(src, dst, recv.at[places["d4"] + own_half]).start()
 
+    ins[4].wait()
+    ins[5].wait()
+    weff[...] = jnp.where(wm[...] != 0, w[...].astype(F32), 0.0).astype(BF)
     loop(0, 2 * n, lambda m: arrived("a4", m, a2_like))
+
+    chunk_rows = 2 * piece_rows
+    wl[...] = jnp.zeros_like(wl)
+    deep = 2 * side // chunk_rows
+
+    def weight_step(i):
+        at = pl.ds(i * deep, deep)
+        left_side = pj[at].reshape(deep * chunk_rows, width)
+        right_side = pb[at].reshape(deep * chunk_rows, width)
+        wl[...] += lax.dot_general(
+            left_side, right_side, (((0,), (0,)), ((), ())), preferred_element_type=F32
+        )
+
+    loop(0, 4 * n // deep, weight_step)
+    yb[:, chunk_rows:] = wl[...].astype(BF).reshape(reps, width // reps, width)
 
     for t in range(tiles):
         _, _, kt, jt = picks[t]
-        rs[t] = pj[pl.ds(jt * ppt, ppt), kt].reshape(side, width)
+        rsf[t] = pj[pl.ds(jt * ppt, ppt), kt].reshape(side, width)
+    rs[...] = (
+        jnp.dot(rsf[...].reshape(tiles * side, width), weff[...], preferred_element_type=F32)
+        .astype(BF)
+        .reshape(tiles, side, width)
+    )
 
     chunks_pair = 2 * side // (2 * piece_rows)
     pairs_half = block // 2 // (2 * side)
@@ -287,7 +305,7 @@
                 cond = jnp.logical_and(live, it == 2 * u + h)
                 lhs[h * side:(h + 1) * side, t * side:(t + 1) * side] = chosen(cond, mk[t])
         total = jnp.dot(lhs[...], rs[...].reshape(tiles * side, width), preferred_element_type=F32)
-        yb[pl.ds(u * chunks_pair, chunks_pair)] = total.astype(BF).reshape(
+        yb[pl.ds(u * chunks_pair, chunks_pair), 0:chunk_rows] = total.astype(BF).reshape(
             chunks_pair, 2 * piece_rows, width
         )
 
@@ -338,64 +356,64 @@
         c2o[...] += c2r[yy].astype(F32)
 
     loop(1, n, c2_add)
-    oc[rep] = c2o[...].astype(BF)
+
+    wz[z] = c2o[chunk_rows:]
+
+    def wz_step(o):
+        zz = around(z, o)
+        copy("wz", zz, z, wz.at[z], wz.at[z], row_of(zz, xl, c), rep).start()
+
+    loop(1, n, wz_step)
+    oc[rep] = c2o[0:chunk_rows].astype(BF)
     pass_hi("c4", oc, y)
     loop(1, n, lambda o: pass_y("c3", oc, o))
 
-    for t in range(tiles):
-        live = picks[t][0]
+    def edge_tile(t):
         scores = lax.dot_general(gs[t], rs[t], (((1,), (1,)), ((), ())), preferred_element_type=F32)
-        ge[t] = chosen(live, tv[t].astype(F32) * scores)
+        ge[t] = chosen(picks[t][0], tv[t].astype(F32) * scores)
+
+    for t in range(tiles // 2):
+        edge_tile(t)
+
+    loop(1, n, lambda o: arrived("wz", around(z, o), wz.at[z]))
+    spot = xl * 2 + c
+    wc[spot] = functools.reduce(jnp.add, [wz[i] for i in range(n)])
+    for r, s in (
+        (core_row, xl * 2 + 1 - c), (lo_row, (1 - xl) * 2 + c), (both_row, (1 - xl) * 2 + 1 - c)
+    ):
+        copy("wc", s, spot, wc.at[spot], wc.at[spot], r, rep).start()
+
+    for t in range(tiles // 2, tiles):
+        edge_tile(t)
     outs = [pltpu.make_async_copy(ge, ge_h, local.at[0])]
     outs[-1].start()
-    cpt = side // (2 * piece_rows)
-    for i in range(per_side):
-        rows = feats[i * cpt:(i + 1) * cpt].reshape(side, width)
-        ft[:, i * side:(i + 1) * side] = rows.astype(F32).T.astype(BF)
+
+    for i in range(1, 4):
+        arrived("wc", lax.rem(spot + i, 4), wc.at[spot])
+    wa[rep] = (wc[0] + wc[1]) + (wc[2] + wc[3])
+    pass_hi("wx", wa, y)
+    loop(1, n, lambda o: pass_y("wy", wa, o))
+
+    loop(1, n, lambda o: relay("c3", "c4", oc, o))
 
     loop(0, n, lambda yy: arrived("d6", yy, gc.at[rep]))
-    grad_cols = gc[...].reshape(block, width)
-    wp[...] = jnp.dot(ft[...], grad_cols, preferred_element_type=F32).reshape(wp.shape)
-    wz[z] = wp[rep]
-
-    def wz_step(o):
-        zz = around(z, o)
-        copy("wz", zz, z, wz.at[z], wz.at[z], row_of(zz, xl, c), rep).start()
-
-    loop(1, n, wz_step)
-    loop(1, n, lambda o: relay("c3", "c4", oc, o))
-
     fg[...] = lax.dot_general(
         gc[...].reshape(block, width), weff[...], (((1,), (1,)), ((), ())), preferred_element_type=F32
     ).astype(BF)
     outs.append(pltpu.make_async_copy(fg, fg_h, local.at[1]))
     outs[-1].start()
 
-    loop(1, n, lambda o: arrived("wz", around(z, o), wz.at[z]))
-    spot = xl * 2 + c
-    wc[spot] = functools.reduce(jnp.add, [wz[i] for i in range(n)])
-    for i, (r, s) in enumerate(
-        ((core_row, xl * 2 + 1 - c), (lo_row, (1 - xl) * 2 + c), (both_row, (1 - xl) * 2 + 1 - c))
-    ):
-        copy("wc", s, spot, wc.at[spot], wc.at[spot], r, rep).start()
-
+    loop(1, n, lambda o: relay("wy", "wx", wa, o))
     loop(0, n, lambda yy: arrived("c4", yy, oc.at[rep]))
     outs.append(pltpu.make_async_copy(oc, out_h, local.at[2]))
     outs[-1].start()
-
-    for i in range(1, 4):
-        arrived("wc", lax.rem(spot + i, 4), wc.at[spot])
-    wa[rep] = (wc[0] + wc[1]) + (wc[2] + wc[3])
-    pass_hi("wx", wa, y)
-    loop(1, n, lambda o: pass_y("wy", wa, o))
-    loop(1, n, lambda o: relay("wy", "wx", wa, o))
     loop(0, n, lambda yy: arrived("wx", yy, wa.at[rep]))
     wgo[...] = jnp.where(wm[...] != 0, wa[...].reshape(width, width), 0.0)
     outs.append(pltpu.make_async_copy(wgo, wg_h, local.at[3]))
     outs[-1].start()
 
     for k in range(2):
-        pl.when(jnp.logical_not(is_me(part_rows[k], group)))(functools.partial(left, "a1", k, a1s.at[0]))
+        pl.when(jnp.logical_not(is_me(part_rows[k], group)))(functools.partial(left, "a1", k, chunk.at[0]))
         pl.when(jnp.logical_not(is_me(owner_rows[k], owner_rep)))(
             functools.partial(left, "d4", k, d4s.at[0])
         )
@@ -409,7 +427,7 @@
     def along_y(o):
         yy = around(y, o)
         left("d5", yy, gc.at[rep])
-        left("c2", yy, oc.at[rep])
+        left("c2", yy, c2s.at[yy])
         left("c3", yy, oc.at[rep])
         left("wy", yy, wa.at[rep])
 
@@ -417,7 +435,7 @@
         left("a3", i, a2_like)
         left("d2", i, a2_like)
         left("d6", i, gc.at[rep])
-        left("c1", i, oc.at[rep])
+        left("c1", i, c1r.at[i])
         left("c4", i, oc.at[rep])
         left("wx", i, wa.at[rep])
 
@@ -433,6 +451,34 @@
         left("wc", lax.rem(spot + i, 4), wc.at[spot])
     for out in outs:
         out.wait()
+
+
+def settle_kernel(*refs):
+    ins, outs, held = refs[:4], refs[4:8], refs[8:12]
+    sem = refs[12]
+    loads = [pltpu.make_async_copy(ins[i], held[i], sem.at[i]) for i in range(4)]
+    stores = [pltpu.make_async_copy(held[i], outs[i], sem.at[4 + i]) for i in range(4)]
+    for one in loads:
+        one.start()
+    for load, store in zip(loads, stores):
+        load.wait()
+        store.start()
+    for one in stores:
+        one.wait()
+
+
+def settle(*arrays):
+    anywhere = pl.BlockSpec(memory_space=pl.ANY)
+    return pl.pallas_call(
+        settle_kernel,
+        out_shape=tuple(jax.ShapeDtypeStruct(a.shape, a.dtype) for a in arrays),
+        in_specs=[anywhere] * 4,
+        out_specs=(anywhere,) * 4,
+        scratch_shapes=[pltpu.VMEM(a.shape, a.dtype) for a in arrays]
+        + [pltpu.SemaphoreType.DMA((8,))],
+        compiler_params=pltpu.CompilerParams(vmem_limit_bytes=VMEM_MIB * 1024 * 1024),
+        name="settle",
+    )(*arrays)
 
 
 def on_device(feats, weight, weight_mask, tile_vals, edge_mask, tile_pos, grad_out):
@@ -445,22 +491,23 @@
     places, total = semaphore_places(n)
     chunked = (reps, 2 * rows, width)
     piece = (2, rows, width)
+    wider = (2 * rows + share, width)
 
     def vm(shape, kind=BF):
         return pltpu.VMEM(shape, kind)
 
     scratch = [
-        vm(chunked), vm((block // side, side, width)), vm((width, width)), vm((width, width), jnp.int32),
+        vm(piece), vm((block // side, side, width)), vm((width, width)), vm((width, width), jnp.int32),
         vm((tiles, side, side)), vm((tiles, side, side), F32),
-        vm((width, width)), vm(piece), vm((4 * n,) + piece),
+        vm((width, width)), vm((4 * n,) + piece),
         vm((tiles, side, side)), vm((tiles, side, side)),
-        vm((tiles, side, width)), vm((tiles, side, width)),
+        vm((tiles, side, width)), vm((tiles, side, width)), vm((tiles, side, width)),
         vm((2 * side, tiles * side)), vm((4 * n,) + piece),
         vm((2 * n,) + piece), vm((n,) + piece), vm((n,) + piece), vm((n,) + piece), vm((n,) + piece),
         vm(piece, F32), vm(piece), vm((reps,) + piece),
-        vm(chunked), vm((n,) + chunked[1:]), vm((n,) + chunked[1:]), vm((n,) + chunked[1:]),
-        vm(chunked[1:], F32), vm(chunked),
-        vm((width, block)), vm((reps, share, width), F32), vm((n, share, width), F32),
+        vm((reps,) + wider), vm((n,) + wider), vm((n,) + wider), vm((n,) + wider),
+        vm(wider, F32), vm(chunked),
+        vm((width, width), F32), vm((n, share, width), F32),
         vm((4, share, width), F32), vm((reps, share, width), F32), vm((width, width), F32),
         vm((tiles, side, side), F32), vm((block, width)),
         pltpu.SemaphoreType.DMA((total,)), pltpu.SemaphoreType.DMA((total,)),
@@ -479,7 +526,7 @@
         out_specs=(anywhere,) * 4,
         scratch_shapes=scratch,
         compiler_params=pltpu.CompilerParams(
-            collective_id=0, has_side_effects=True, vmem_limit_bytes=40 * 1024 * 1024
+            collective_id=0, has_side_effects=True, vmem_limit_bytes=VMEM_MIB * 1024 * 1024
         ),
         cost_estimate=pl.CostEstimate(
             flops=3_000_000_000, bytes_accessed=5_000_000, transcendentals=0
@@ -487,14 +534,14 @@
         name="layer",
     )(
         tile_pos,
-        feats.reshape(chunked),
+        feats.reshape((reps,) + piece),
         grad_out.reshape(block // side, side, width),
         weight,
         weight_mask,
         tile_vals,
         edge_mask,
     )
-    return out.reshape(block, width), fgrad, wgrad, edge
+    return settle(out.reshape(block, width), fgrad, wgrad, edge)
 
 
 def solution(mesh):

time: 99.8 us -> 88.6 us (0.89)
  local copies, waits for them, and re-layouts: 9.88 us -> 0 us
    unnamed x18 -> x0, local copies, waits for them, and re-layouts: 9.88 us -> none
    pallas_call x1, Pallas kernels: 87.9 us -> 84.8 us  [on_device(): pl.pallas_call(functools.partial(kernel, n, places), out_shape=(jax.Shape...]
    pallas_call x0 -> x1, Pallas kernels: none -> 2.48 us  [settle(): pl.pallas_call(settle_kernel, out_shape=tuple((jax.ShapeDtypeStruct(a.sha...]
where the time goes in v4:
time: 88.6 us; the launch traced here: 87.9 us
  Pallas kernels  87.3 us (99%)
    pallas_call x1, Pallas kernels, on_device(): pl.pallas_call(functools.partial(kernel, n, places), out_shape=(jax.Shape...  84.8 us
    pallas_call x1, Pallas kernels, settle(): pl.pallas_call(settle_kernel, out_shape=tuple((jax.ShapeDtypeStruct(a.sha...  2.48 us

profile of v4, /device:TPU:1, one launch (start us, length us, event | category | flops | bytes accessed | tf_op | source)
XLA Modules:
  0.0 87.9 jit_solution(17332789393314111920)
XLA Ops:
  0.6 84.8 %layer.1 = (bf16[16,64,256]{2,1,0:T(8,128)(2,1)}, bf16[1024,256]{1,0:T(8,128)(2,1)}, f32[256,256]{1,0:T(8,128)}, f32[12,128,128]{2,1,0:T(8,128)}) custom-call(s32[12]{0:T(128)} %pos_ref.1, bf16[16,2,32,256]{3,2,1,0:T(8,128)(2,1)} %bitcast.4, bf16[8,128,256]{2,1,0:T(8,128)(2,1)} %bitcast.5, bf16[256,256]{1,0:T(8,128)(2,1)} %w_h.1, s32[256,256]{1,0:T(8,128)} %wm_h.1, ...), custom_call_target="tpu_custom_call" | custom-call | flops 3000000000 | bytes 5000000 | tf_op jit(solution)/shard_map/layer/pallas_call | solution.py:517
  85.4 2.5 %settle.1 = (bf16[1024,256]{1,0:T(8,128)(2,1)}, bf16[1024,256]{1,0:T(8,128)(2,1)}, f32[256,256]{1,0:T(8,128)}, f32[12,128,128]{2,1,0:T(8,128)}) custom-call(bf16[1024,256]{1,0:T(8,128)(2,1)} %bitcast.3, bf16[1024,256]{1,0:T(8,128)(2,1)} %get-tuple-element.9.refs_1_, f32[256,256]{1,0:T(8,128)} %get-tuple-element.10.refs_2_, ...), custom_call_target="tpu_custom_call" | custom-call | tf_op jit(solution)/shard_map/settle/pallas_call | solution.py:472

commit v5 on v4

--- a/solution.py
+++ b/solution.py
@@ -17,7 +17,7 @@
         a1=2, a2=n, a3=n, a4=2 * n,
         d1=2 * n, d2=n, d3=n, d4=2, d5=n, d6=n,
         c1=n, c2=n, c3=n, c4=n,
-        wz=n, wc=4, wy=n, wx=n,
+        v1=1, v2=n, wz=n, wc=4, wy=n, wx=n,
     )
     places, total = {}, 0
     for name, count in counts.items():
@@ -42,7 +42,7 @@
     weff, pj, mk, mkt, gs, rsf, rs, lhs, pb,
     d1r, d2s, d2r, d3s, d3r, d3o, d4s, gc,
     yb, c1r, c2s, c2r, c2o, oc,
-    wl, wz, wc, wa, wgo, ge, fg,
+    pbt, lf, wl, wv, v1r, v2s, v2r, wz, wc, wa, wgo, ge, fg,
     send, recv, local,
 ):
     row, rep = lax.axis_index("row"), lax.axis_index("rep")
@@ -217,6 +217,22 @@
 
     loop(1, n + 1, d2_step)
 
+    chunk_rows = 2 * piece_rows
+    deep = 2 * side // chunk_rows
+
+    def turn(i):
+        rows = pb[pl.ds(i * deep, deep)].reshape(2 * side, width)
+        pbt[i] = rows.astype(F32).T.astype(BF)
+
+    loop(0, 4 * n // deep, turn)
+
+    def spread_row(i):
+        for t in range(tiles):
+            cond = jnp.logical_and(picks[t][0], picks[t][1] == i)
+            lf[i, :, t * side:(t + 1) * side] = chosen(cond, mk[t])
+
+    loop(0, per_side, spread_row)
+
     def a2_step(o):
         zz = around(z, o)
         arrived("a2", zz, a2_like)
@@ -225,6 +241,13 @@
 
     a2_like = pj.at[mine]
     loop(1, n, a2_step)
+
+    def a3_step(o):
+        zz = around(z, o)
+        arrived("a3", zz, a2_like)
+        pass_core((1 - xl) * n + zz)
+
+    loop(0, n, a3_step)
 
     def d3_sum(zz):
         m = xl * n + zz
@@ -240,51 +263,21 @@
     loop(1, n, d3_step)
     d3o[...] = d3_sum(z)
 
-    def a3_step(o):
-        zz = around(z, o)
-        arrived("a3", zz, a2_like)
-        pass_core((1 - xl) * n + zz)
-
-    loop(0, n, a3_step)
-
-    def d3_add(o):
-        zz = around(z, o)
-        arrived("d3", zz, d3r.at[zz])
-        d3o[...] += d3r[zz].astype(F32)
-
-    loop(1, n, d3_add)
-    d4s[...] = d3o[...].astype(BF)
-    for k in range(2):
-        same = is_me(owner_rows[k], owner_rep)
-        src, dst = d4s.at[k], gc.at[owner_rep, own_half]
-
-        @pl.when(jnp.logical_not(same))
-        def _(src=src, dst=dst, k=k):
-            copy("d4", k, own_half, src, dst, owner_rows[k], owner_rep).start()
-
-        @pl.when(same)
-        def _(src=src, dst=dst):
-            pltpu.make_async_copy(src, dst, recv.at[places["d4"] + own_half]).start()
-
     ins[4].wait()
     ins[5].wait()
     weff[...] = jnp.where(wm[...] != 0, w[...].astype(F32), 0.0).astype(BF)
     loop(0, 2 * n, lambda m: arrived("a4", m, a2_like))
 
-    chunk_rows = 2 * piece_rows
     wl[...] = jnp.zeros_like(wl)
-    deep = 2 * side // chunk_rows
 
     def weight_step(i):
-        at = pl.ds(i * deep, deep)
-        left_side = pj[at].reshape(deep * chunk_rows, width)
-        right_side = pb[at].reshape(deep * chunk_rows, width)
-        wl[...] += lax.dot_general(
-            left_side, right_side, (((0,), (0,)), ((), ())), preferred_element_type=F32
-        )
+        rows = pj[pl.ds(i * deep, deep)].reshape(2 * side, width)
+        wl[...] += jnp.dot(pbt[i], rows, preferred_element_type=F32)
 
     loop(0, 4 * n // deep, weight_step)
-    yb[:, chunk_rows:] = wl[...].astype(BF).reshape(reps, width // reps, width)
+    wv[...] = wl[...].T.astype(BF).reshape(wv.shape)
+    away = wv.at[pl.ds((1 - xh) * n, n)]
+    copy("v1", 0, 0, away, v1r, row, hi_rep).start()
 
     for t in range(tiles):
         _, _, kt, jt = picks[t]
@@ -299,13 +292,9 @@
     pairs_half = block // 2 // (2 * side)
 
     def forward_pair(u):
-        for h in range(2):
-            for t in range(tiles):
-                live, it, _, _ = picks[t]
-                cond = jnp.logical_and(live, it == 2 * u + h)
-                lhs[h * side:(h + 1) * side, t * side:(t + 1) * side] = chosen(cond, mk[t])
-        total = jnp.dot(lhs[...], rs[...].reshape(tiles * side, width), preferred_element_type=F32)
-        yb[pl.ds(u * chunks_pair, chunks_pair), 0:chunk_rows] = total.astype(BF).reshape(
+        mine_rows = lf[pl.ds(2 * u, 2)].reshape(2 * side, tiles * side)
+        total = jnp.dot(mine_rows, rs[...].reshape(tiles * side, width), preferred_element_type=F32)
+        yb[pl.ds(u * chunks_pair, chunks_pair)] = total.astype(BF).reshape(
             chunks_pair, 2 * piece_rows, width
         )
 
@@ -317,6 +306,25 @@
 
     loop(1, n + 1, c1_step)
     loop(0, pairs_half, lambda i: forward_pair(xh * pairs_half + i))
+
+    def d3_add(o):
+        zz = around(z, o)
+        arrived("d3", zz, d3r.at[zz])
+        d3o[...] += d3r[zz].astype(F32)
+
+    loop(1, n, d3_add)
+    d4s[...] = d3o[...].astype(BF)
+    for k in range(2):
+        same = is_me(owner_rows[k], owner_rep)
+        src, dst = d4s.at[k], gc.at[owner_rep, own_half]
+
+        @pl.when(jnp.logical_not(same))
+        def _(src=src, dst=dst, k=k):
+            copy("d4", k, own_half, src, dst, owner_rows[k], owner_rep).start()
+
+        @pl.when(same)
+        def _(src=src, dst=dst):
+            pltpu.make_async_copy(src, dst, recv.at[places["d4"] + own_half]).start()
 
     def pass_hi(name, ref, yy):
         at = xh * n + yy
@@ -325,24 +333,46 @@
     def pass_y(name, ref, o):
         yy = around(y, o)
         copy(name, yy, y, ref.at[rep], ref.at[rep], row, xh * n + yy).start()
+
+    copy("v1", 0, 0, away, v1r, row, hi_rep).wait_recv()
+
+    def v2_step(o):
+        yy = around(y, o)
+        v2s[yy] = (wv[xh * n + yy].astype(F32) + v1r[yy].astype(F32)).astype(BF)
+        copy("v2", yy, y, v2s.at[yy], v2r.at[y], row, xh * n + yy).start()
+
+    loop(1, n, v2_step)
+    wz[z] = wv[rep].astype(F32) + v1r[y].astype(F32)
+
+    def c2_sum(yy):
+        arrived("c1", yy, c1r.at[yy])
+        return yb[xh * n + yy].astype(F32) + c1r[yy].astype(F32)
+
+    def c2_step(o):
+        yy = around(y, o)
+        c2s[yy] = c2_sum(yy).astype(BF)
+        copy("c2", yy, y, c2s.at[yy], c2r.at[y], row, xh * n + yy).start()
+
+    loop(1, n, c2_step)
+    c2o[...] = c2_sum(y)
 
     arrived("d4", 0, d4s.at[0])
     arrived("d4", 1, d4s.at[0])
     pass_hi("d6", gc, y)
     loop(1, n, lambda o: pass_y("d5", gc, o))
 
-    def c2_sum(yy):
-        arrived("c1", yy, c1r.at[yy])
-        return yb[xh * n + yy].astype(F32) + c1r[yy].astype(F32)
-
-    def c2_step(o):
-        yy = around(y, o)
-        c2s[yy] = c2_sum(yy).astype(BF)
-        copy("c2", yy, y, c2s.at[yy], c2r.at[y], row, xh * n + yy).start()
-
-    loop(1, n, c2_step)
-    c2o[...] = c2_sum(y)
-
+    def v2_add(o):
+        yy = around(y, o)
+        arrived("v2", yy, v2r.at[yy])
+        wz[z] += v2r[yy].astype(F32)
+
+    loop(1, n, v2_add)
+
+    def wz_step(o):
+        zz = around(z, o)
+        copy("wz", zz, z, wz.at[z], wz.at[z], row_of(zz, xl, c), rep).start()
+
+    loop(1, n, wz_step)
     def relay(got, gone, ref, o):
         yy = around(y, o)
         arrived(got, yy, ref.at[rep])
@@ -357,14 +387,7 @@
 
     loop(1, n, c2_add)
 
-    wz[z] = c2o[chunk_rows:]
-
-    def wz_step(o):
-        zz = around(z, o)
-        copy("wz", zz, z, wz.at[z], wz.at[z], row_of(zz, xl, c), rep).start()
-
-    loop(1, n, wz_step)
-    oc[rep] = c2o[0:chunk_rows].astype(BF)
+    oc[rep] = c2o[...].astype(BF)
     pass_hi("c4", oc, y)
     loop(1, n, lambda o: pass_y("c3", oc, o))
 
@@ -428,6 +451,7 @@
         yy = around(y, o)
         left("d5", yy, gc.at[rep])
         left("c2", yy, c2s.at[yy])
+        left("v2", yy, v2s.at[yy])
         left("c3", yy, oc.at[rep])
         left("wy", yy, wa.at[rep])
 
@@ -449,6 +473,7 @@
     loop(0, 2 * n, cores)
     for i in range(1, 4):
         left("wc", lax.rem(spot + i, 4), wc.at[spot])
+    left("v1", 0, v1r)
     for out in outs:
         out.wait()
 
@@ -491,7 +516,7 @@
     places, total = semaphore_places(n)
     chunked = (reps, 2 * rows, width)
     piece = (2, rows, width)
-    wider = (2 * rows + share, width)
+    slices = (share, width)
 
     def vm(shape, kind=BF):
         return pltpu.VMEM(shape, kind)
@@ -505,9 +530,11 @@
         vm((2 * side, tiles * side)), vm((4 * n,) + piece),
         vm((2 * n,) + piece), vm((n,) + piece), vm((n,) + piece), vm((n,) + piece), vm((n,) + piece),
         vm(piece, F32), vm(piece), vm((reps,) + piece),
-        vm((reps,) + wider), vm((n,) + wider), vm((n,) + wider), vm((n,) + wider),
-        vm(wider, F32), vm(chunked),
-        vm((width, width), F32), vm((n, share, width), F32),
+        vm(chunked), vm((n,) + chunked[1:]), vm((n,) + chunked[1:]), vm((n,) + chunked[1:]),
+        vm(chunked[1:], F32), vm(chunked),
+        vm((2 * block // (2 * side), width, 2 * side)), vm((block // side, side, tiles * side)),
+        vm((width, width), F32), vm((reps,) + slices), vm((n,) + slices), vm((n,) + slices), vm((n,) + slices),
+        vm((n,) + slices, F32),
         vm((4, share, width), F32), vm((reps, share, width), F32), vm((width, width), F32),
         vm((tiles, side, side), F32), vm((block, width)),
         pltpu.SemaphoreType.DMA((total,)), pltpu.SemaphoreType.DMA((total,)),

time: 88.6 us -> 86.5 us (0.976)
  Pallas kernels: 87.3 us -> 84.5 us
    pallas_call x1, Pallas kernels: 84.8 us -> 82 us  [on_device(): pl.pallas_call(functools.partial(kernel, n, places), out_shape=(jax.Shape...]
where the time goes in v5:
time: 86.5 us; the launch traced here: 85.1 us
  Pallas kernels  84.5 us (98%)
    pallas_call x1, Pallas kernels, on_device(): pl.pallas_call(functools.partial(kernel, n, places), out_shape=(jax.Shape...  82 us
    pallas_call x1, Pallas kernels, settle(): pl.pallas_call(settle_kernel, out_shape=tuple((jax.ShapeDtypeStruct(a.sha...  2.48 us

profile of v5, /device:TPU:1, one launch (start us, length us, event | category | flops | bytes accessed | tf_op | source)
XLA Modules:
  0.0 85.1 jit_solution(10116687661002910122)
XLA Ops:
  0.6 82.0 %layer.1 = (bf16[16,64,256]{2,1,0:T(8,128)(2,1)}, bf16[1024,256]{1,0:T(8,128)(2,1)}, f32[256,256]{1,0:T(8,128)}, f32[12,128,128]{2,1,0:T(8,128)}) custom-call(s32[12]{0:T(128)} %pos_ref.1, bf16[16,2,32,256]{3,2,1,0:T(8,128)(2,1)} %bitcast.4, bf16[8,128,256]{2,1,0:T(8,128)(2,1)} %bitcast.5, bf16[256,256]{1,0:T(8,128)(2,1)} %w_h.1, s32[256,256]{1,0:T(8,128)} %wm_h.1, ...), custom_call_target="tpu_custom_call" | custom-call | flops 3000000000 | bytes 5000000 | tf_op jit(solution)/shard_map/layer/pallas_call | solution.py:544
  82.6 2.5 %settle.1 = (bf16[1024,256]{1,0:T(8,128)(2,1)}, bf16[1024,256]{1,0:T(8,128)(2,1)}, f32[256,256]{1,0:T(8,128)}, f32[12,128,128]{2,1,0:T(8,128)}) custom-call(bf16[1024,256]{1,0:T(8,128)(2,1)} %bitcast.3, bf16[1024,256]{1,0:T(8,128)(2,1)} %get-tuple-element.9.refs_1_, f32[256,256]{1,0:T(8,128)} %get-tuple-element.10.refs_2_, ...), custom_call_target="tpu_custom_call" | custom-call | tf_op jit(solution)/shard_map/settle/pallas_call | solution.py:497

commit v6 on v5

--- a/solution.py
+++ b/solution.py
@@ -242,13 +242,6 @@
     a2_like = pj.at[mine]
     loop(1, n, a2_step)
 
-    def a3_step(o):
-        zz = around(z, o)
-        arrived("a3", zz, a2_like)
-        pass_core((1 - xl) * n + zz)
-
-    loop(0, n, a3_step)
-
     def d3_sum(zz):
         m = xl * n + zz
         arrived("d1", m, d1r.at[m])
@@ -262,6 +255,13 @@
 
     loop(1, n, d3_step)
     d3o[...] = d3_sum(z)
+
+    def a3_step(o):
+        zz = around(z, o)
+        arrived("a3", zz, a2_like)
+        pass_core((1 - xl) * n + zz)
+
+    loop(0, n, a3_step)
 
     ins[4].wait()
     ins[5].wait()
@@ -305,7 +305,6 @@
         copy("c1", yy, yy, yb.at[(1 - xh) * n + yy], c1r.at[yy], row, hi_rep).start()
 
     loop(1, n + 1, c1_step)
-    loop(0, pairs_half, lambda i: forward_pair(xh * pairs_half + i))
 
     def d3_add(o):
         zz = around(z, o)
@@ -326,6 +325,8 @@
         def _(src=src, dst=dst):
             pltpu.make_async_copy(src, dst, recv.at[places["d4"] + own_half]).start()
 
+    loop(0, pairs_half, lambda i: forward_pair(xh * pairs_half + i))
+
     def pass_hi(name, ref, yy):
         at = xh * n + yy
         copy(name, yy, yy, ref.at[at], ref.at[at], row, hi_rep).start()
@@ -378,7 +379,6 @@
         arrived(got, yy, ref.at[rep])
         pass_hi(gone, ref, yy)
 
-    loop(1, n, lambda o: relay("d5", "d6", gc, o))
 
     def c2_add(o):
         yy = around(y, o)
@@ -405,6 +405,8 @@
         (core_row, xl * 2 + 1 - c), (lo_row, (1 - xl) * 2 + c), (both_row, (1 - xl) * 2 + 1 - c)
     ):
         copy("wc", s, spot, wc.at[spot], wc.at[spot], r, rep).start()
+
+    loop(1, n, lambda o: relay("d5", "d6", gc, o))
 
     for t in range(tiles // 2, tiles):
         edge_tile(t)

time: 86.5 us -> 82.7 us (0.956)
  Pallas kernels: 84.5 us -> 80.5 us
    pallas_call x1, Pallas kernels: 82 us -> 78.1 us  [on_device(): pl.pallas_call(functools.partial(kernel, n, places), out_shape=(jax.Shape...]
where the time goes in v6:
time: 82.7 us; the launch traced here: 81.2 us
  Pallas kernels  80.5 us (97%)
    pallas_call x1, Pallas kernels, on_device(): pl.pallas_call(functools.partial(kernel, n, places), out_shape=(jax.Shape...  78.1 us
    pallas_call x1, Pallas kernels, settle(): pl.pallas_call(settle_kernel, out_shape=tuple((jax.ShapeDtypeStruct(a.sha...  2.48 us

profile of v6, /device:TPU:1, one launch (start us, length us, event | category | flops | bytes accessed | tf_op | source)
XLA Modules:
  0.0 81.2 jit_solution(9356438729390150766)
XLA Ops:
  0.6 78.1 %layer.1 = (bf16[16,64,256]{2,1,0:T(8,128)(2,1)}, bf16[1024,256]{1,0:T(8,128)(2,1)}, f32[256,256]{1,0:T(8,128)}, f32[12,128,128]{2,1,0:T(8,128)}) custom-call(s32[12]{0:T(128)} %pos_ref.1, bf16[16,2,32,256]{3,2,1,0:T(8,128)(2,1)} %bitcast.4, bf16[8,128,256]{2,1,0:T(8,128)(2,1)} %bitcast.5, bf16[256,256]{1,0:T(8,128)(2,1)} %w_h.1, s32[256,256]{1,0:T(8,128)} %wm_h.1, ...), custom_call_target="tpu_custom_call" | custom-call | flops 3000000000 | bytes 5000000 | tf_op jit(solution)/shard_map/layer/pallas_call | solution.py:546
  78.7 2.5 %settle.1 = (bf16[1024,256]{1,0:T(8,128)(2,1)}, bf16[1024,256]{1,0:T(8,128)(2,1)}, f32[256,256]{1,0:T(8,128)}, f32[12,128,128]{2,1,0:T(8,128)}) custom-call(bf16[1024,256]{1,0:T(8,128)(2,1)} %bitcast.3, bf16[1024,256]{1,0:T(8,128)(2,1)} %get-tuple-element.9.refs_1_, f32[256,256]{1,0:T(8,128)} %get-tuple-element.10.refs_2_, ...), custom_call_target="tpu_custom_call" | custom-call | tf_op jit(solution)/shard_map/settle/pallas_call | solution.py:499

commit v7 on v6

--- a/solution.py
+++ b/solution.py
@@ -357,23 +357,24 @@
     loop(1, n, c2_step)
     c2o[...] = c2_sum(y)
 
+    def v2_add(o):
+        yy = around(y, o)
+        arrived("v2", yy, v2r.at[yy])
+        wz[z] += v2r[yy].astype(F32)
+
+    loop(1, n, v2_add)
+
+    def wz_step(o):
+        zz = around(z, o)
+        copy("wz", zz, z, wz.at[z], wz.at[z], row_of(zz, xl, c), rep).start()
+
+    loop(1, n, wz_step)
+
     arrived("d4", 0, d4s.at[0])
     arrived("d4", 1, d4s.at[0])
     pass_hi("d6", gc, y)
     loop(1, n, lambda o: pass_y("d5", gc, o))
 
-    def v2_add(o):
-        yy = around(y, o)
-        arrived("v2", yy, v2r.at[yy])
-        wz[z] += v2r[yy].astype(F32)
-
-    loop(1, n, v2_add)
-
-    def wz_step(o):
-        zz = around(z, o)
-        copy("wz", zz, z, wz.at[z], wz.at[z], row_of(zz, xl, c), rep).start()
-
-    loop(1, n, wz_step)
     def relay(got, gone, ref, o):
         yy = around(y, o)
         arrived(got, yy, ref.at[rep])
@@ -384,19 +385,6 @@
         yy = around(y, o)
         arrived("c2", yy, c2r.at[yy])
         c2o[...] += c2r[yy].astype(F32)
-
-    loop(1, n, c2_add)
-
-    oc[rep] = c2o[...].astype(BF)
-    pass_hi("c4", oc, y)
-    loop(1, n, lambda o: pass_y("c3", oc, o))
-
-    def edge_tile(t):
-        scores = lax.dot_general(gs[t], rs[t], (((1,), (1,)), ((), ())), preferred_element_type=F32)
-        ge[t] = chosen(picks[t][0], tv[t].astype(F32) * scores)
-
-    for t in range(tiles // 2):
-        edge_tile(t)
 
     loop(1, n, lambda o: arrived("wz", around(z, o), wz.at[z]))
     spot = xl * 2 + c
@@ -405,6 +393,19 @@
         (core_row, xl * 2 + 1 - c), (lo_row, (1 - xl) * 2 + c), (both_row, (1 - xl) * 2 + 1 - c)
     ):
         copy("wc", s, spot, wc.at[spot], wc.at[spot], r, rep).start()
+
+    loop(1, n, c2_add)
+
+    oc[rep] = c2o[...].astype(BF)
+    pass_hi("c4", oc, y)
+    loop(1, n, lambda o: pass_y("c3", oc, o))
+
+    def edge_tile(t):
+        scores = lax.dot_general(gs[t], rs[t], (((1,), (1,)), ((), ())), preferred_element_type=F32)
+        ge[t] = chosen(picks[t][0], tv[t].astype(F32) * scores)
+
+    for t in range(tiles // 2):
+        edge_tile(t)
 
     loop(1, n, lambda o: relay("d5", "d6", gc, o))
 

time: 82.7 us -> 82.2 us (level)
  no operation moved by 1% of the time
where the time goes in v7:
time: 82.2 us; the launch traced here: 80.8 us
  Pallas kernels  80.2 us (98%)
    pallas_call x1, Pallas kernels, on_device(): pl.pallas_call(functools.partial(kernel, n, places), out_shape=(jax.Shape...  77.7 us
    pallas_call x1, Pallas kernels, settle(): pl.pallas_call(settle_kernel, out_shape=tuple((jax.ShapeDtypeStruct(a.sha...  2.48 us

profile of v7, /device:TPU:1, one launch (start us, length us, event | category | flops | bytes accessed | tf_op | source)
XLA Modules:
  0.0 80.8 jit_solution(9155244108237658038)
XLA Ops:
  0.6 77.7 %layer.1 = (bf16[16,64,256]{2,1,0:T(8,128)(2,1)}, bf16[1024,256]{1,0:T(8,128)(2,1)}, f32[256,256]{1,0:T(8,128)}, f32[12,128,128]{2,1,0:T(8,128)}) custom-call(s32[12]{0:T(128)} %pos_ref.1, bf16[16,2,32,256]{3,2,1,0:T(8,128)(2,1)} %bitcast.4, bf16[8,128,256]{2,1,0:T(8,128)(2,1)} %bitcast.5, bf16[256,256]{1,0:T(8,128)(2,1)} %w_h.1, s32[256,256]{1,0:T(8,128)} %wm_h.1, ...), custom_call_target="tpu_custom_call" | custom-call | flops 3000000000 | bytes 5000000 | tf_op jit(solution)/shard_map/layer/pallas_call | solution.py:547
  78.4 2.5 %settle.1 = (bf16[1024,256]{1,0:T(8,128)(2,1)}, bf16[1024,256]{1,0:T(8,128)(2,1)}, f32[256,256]{1,0:T(8,128)}, f32[12,128,128]{2,1,0:T(8,128)}) custom-call(bf16[1024,256]{1,0:T(8,128)(2,1)} %bitcast.3, bf16[1024,256]{1,0:T(8,128)(2,1)} %get-tuple-element.9.refs_1_, f32[256,256]{1,0:T(8,128)} %get-tuple-element.10.refs_2_, ...), custom_call_target="tpu_custom_call" | custom-call | tf_op jit(solution)/shard_map/settle/pallas_call | solution.py:500
